TPU v7x, 32 devices: a whole 2x2x4 slice. The times are simulated.
32 devices in a mesh: seq: 8 (over z, y), row: 4 (over x, core).
Axes of the slice: x: 2, y: 2, z: 4, core: 2. Of those that a mesh axis runs over, the one named last changes fastest.
Arguments:
- inputs: float32 [8, 1024, 1024], P('row', 'seq'), may hold values from -6 to 6
- cotangent: float32 [8, 1024, 1024], P('row', 'seq'), may hold values from -6 to 6
- segments: int32 [8, 1024], P('row', 'seq'), may hold values from 0 to 4, as said below
- norm1_gain: bfloat16 [1024], P(('seq', 'row')), may hold values from 0.5 to 1.5
- input_proj: bfloat16 [1024, 1536], P(('seq', 'row')), may hold values from -0.1875 to 0.1875
- branch_proj: bfloat16 [1024, 1536], P(('seq', 'row')), may hold values from -0.1875 to 0.1875
- conv_weight: bfloat16 [4, 1536], P(None, ('seq', 'row')), may hold values from -3 to 3
- conv_bias: bfloat16 [1536], P(('seq', 'row')), may hold values from -2 to 2
- recur_gate: bfloat16 [1536, 128], P(('seq', 'row')), may hold values from -0.5 to 0.5
- input_gate: bfloat16 [1536, 128], P(('seq', 'row')), may hold values from -0.5 to 0.5
- recur_bias: bfloat16 [1536], P(('seq', 'row')), may hold values from -2 to 2
- input_bias: bfloat16 [1536], P(('seq', 'row')), may hold values from -2 to 2
- decay_param: bfloat16 [1536], P(('seq', 'row')), may hold values from -16 to -3
- output_proj: bfloat16 [1536, 1024], P(('seq', 'row')), may hold values from -0.4375 to 0.4375
- norm2_gain: bfloat16 [1024], P(('seq', 'row')), may hold values from 0.5 to 1.5
- mlp_gate: bfloat16 [1024, 3072], P(('seq', 'row')), may hold values from -0.1875 to 0.1875
- mlp_up: bfloat16 [1024, 3072], P(('seq', 'row')), may hold values from -0.1875 to 0.1875
- mlp_down: bfloat16 [3072, 1024], P(('seq', 'row')), may hold values from -0.21875 to 0.21875
Outputs:
- result: float32 [8, 1024, 1024], P('row', 'seq')
- grad_inputs: float32 [8, 1024, 1024], P('row', 'seq')
- grad_norm1_gain: float32 [1024], P(('seq', 'row'))
- grad_input_proj: float32 [1024, 1536], P(('seq', 'row'))
- grad_branch_proj: float32 [1024, 1536], P(('seq', 'row'))
- grad_conv_weight: float32 [4, 1536], P(None, ('seq', 'row'))
- grad_conv_bias: float32 [1536], P(('seq', 'row'))
- grad_recur_gate: float32 [1536, 128], P(('seq', 'row'))
- grad_input_gate: float32 [1536, 128], P(('seq', 'row'))
- grad_recur_bias: float32 [1536], P(('seq', 'row'))
- grad_input_bias: float32 [1536], P(('seq', 'row'))
- grad_decay_param: float32 [1536], P(('seq', 'row'))
- grad_output_proj: float32 [1536, 1024], P(('seq', 'row'))
- grad_norm2_gain: float32 [1024], P(('seq', 'row'))
- grad_mlp_gate: float32 [1024, 3072], P(('seq', 'row'))
- grad_mlp_up: float32 [1024, 3072], P(('seq', 'row'))
- grad_mlp_down: float32 [3072, 1024], P(('seq', 'row'))
Inputs may be any that keep to these rules, and one draw needn't show every extreme that they name: `segments`: within a row the numbers never fall and rise by one at each of four document starts. In even rows two documents start among the first 128 tokens and two among the last 128 tokens. In odd rows one starts among the first 128 tokens, one among the last 128, and the two others lie in the token ranges of the two middle indices of seq, each at least 3 tokens after the range's start.
All inputs are finite; a program needn't handle non-finite values.
Results may differ from a plain program's by a relative error of at most 0.014.
Values may be sent and summed in bfloat16 or wider, within the bound.
No kernel may reach another device: no remote copies, remote signals or barrier semaphores. Data moves between devices by JAX's collectives and lax.ppermute only.
A program may use at most 320 MiB of HBM per device.

v0:
```python
import functools
import math

import jax
import jax.numpy as jnp
import numpy as np
from jax import lax
from jax.experimental import pallas as pl
from jax.experimental.pallas import tpu as pltpu
from jax.sharding import Mesh, PartitionSpec as P

EPS = 1e-06
BF = jnp.bfloat16
F32 = jnp.float32
AXES = ("z", "y", "x", "c")
MIB = 1 << 20
TILE = 256
HALO = 8
GELU_C = math.sqrt(2.0 / math.pi)


class Place:
    def __init__(self):
        self.size = {axis: lax.axis_size(axis) for axis in AXES}
        self.at = {axis: lax.axis_index(axis) for axis in AXES}
        nz, ny, nx, _ = self.size.values()
        self.seq, self.row = nz * ny, nx * 2
        self.s = self.at["z"] * ny + self.at["y"]
        self.stride = {"z": ny * self.row, "y": self.row, "x": 2, "c": 1}
        self.chips = nz * ny * nx
        self.sizes = (nz, ny, nx)
        self.where = jnp.stack([self.at[axis] for axis in AXES]).astype(jnp.int32)


    def ring(self, value, axis, shift):
        pairs = []
        for i in range(self.seq * self.row):
            at = (i // self.stride[axis]) % self.size[axis]
            to = (at + shift) % self.size[axis]
            pairs.append((i, i + (to - at) * self.stride[axis]))
        return lax.ppermute(value, AXES, pairs)

    def along(self, value, distance):
        pairs = []
        for s in range(self.seq):
            if 0 <= s + distance < self.seq:
                for r in range(self.row):
                    pairs.append((s * self.row + r, (s + distance) * self.row + r))
        return lax.ppermute(value, AXES, pairs)

    def ordered(self, mine, other):
        high = self.at["c"] != 0
        return jnp.where(high, other, mine), jnp.where(high, mine, other)


class Order:
    def __init__(self, place):
        self.place = place
        self.last = ()
        self.sent = ()

    def tie(self, value):
        if not self.last:
            return value
        return lax.optimization_barrier((value,) + self.last)[0]

    def must(self, *values):
        self.sent += values

    def ring(self, value, axis, shift=1):
        value = self.tie(value)
        self.sent += (value,)
        return self.place.ring(value, axis, shift)

    def along(self, value, distance):
        value = self.tie(value)
        self.sent += (value,)
        return self.place.along(value, distance)

    def wait(self, *values):
        n = len(values)
        held = values + self.last + self.sent
        if len(held) > n:
            values = lax.optimization_barrier(held)[:n]
        self.last = tuple(values)
        self.sent = ()
        return values[0] if n == 1 else values


class Gather:
    def __init__(self, order, value, axis, dim, direct=False, both=False):
        self.order, self.axis, self.dim = order, axis, dim
        self.n = order.place.size[axis]
        self.pieces = [value]
        self.direct = direct
        self.both = both and self.n == 4
        if self.both:
            self.flying = [order.ring(value, axis, 1), order.ring(value, axis, 3)]
            return
        shifts = range(1, self.n) if direct else range(1, min(2, self.n))
        self.flying = [order.ring(value, axis, k) for k in shifts]

    def next(self):
        if self.direct:
            if self.flying:
                got = self.order.wait(*self.flying)
                self.pieces += [got] if len(self.flying) == 1 else list(got)
            self.flying = []
            return
        if self.both:
            if len(self.flying) == 2:
                one, three = self.order.wait(*self.flying)
                self.pieces += [one, None, three]
                self.flying = [self.order.ring(one, self.axis)]
            elif self.flying:
                self.pieces[2] = self.order.wait(self.flying.pop())
            return
        got = self.order.wait(self.flying.pop())
        self.pieces.append(got)
        if len(self.pieces) < self.n:
            self.flying = [self.order.ring(got, self.axis)]

    def arrived(self):
        while len(self.pieces) < self.n or (self.both and self.flying):
            self.next()
        return self.pieces

    def done(self):
        return self.whole(self.arrived())

    def whole(self, pieces):
        at = self.order.place.at[self.axis]
        if self.n == 2:
            high = at != 0
            mine, other = pieces
            parts = [jnp.where(high, other, mine), jnp.where(high, mine, other)]
            return jnp.concatenate(parts, axis=self.dim)
        parts = [
            lax.select_n(lax.rem(at - j + self.n, self.n), *pieces) for j in range(self.n)
        ]
        return jnp.concatenate(parts, axis=self.dim)

    def weight(self, rows):
        if rows % 16 == 0:
            return self.arrived()
        whole = self.done()[..., :rows, :]
        return [whole.reshape(-1, whole.shape[-1])]


class Scatter:
    def __init__(self, order, blocks, axis, direct=False, between=BF, both=False):
        self.order, self.axis, self.blocks = order, axis, list(blocks)
        self.n = order.place.size[axis]
        self.both = both and self.n == 4
        self.direct, self.between = direct, between
        self.hop = 0
        self.held = False
        if self.both:
            self.flying = [order.ring(self.blocks[1], axis, 3), order.ring(self.blocks[2], axis, 1)]
        elif direct:
            self.flying = [
                order.ring(self.blocks[i], axis, self.n - 1 - i) for i in range(self.n - 1)
            ]
        elif self.n > 1:
            self.flying = order.ring(self.blocks[0], axis)

    def next(self):
        if self.both:
            if self.hop == 0:
                far, near = self.order.wait(*self.flying)
                total = far.astype(F32) + self.blocks[0].astype(F32)
                self.got = [near]
                self.flying = self.order.ring(total.astype(self.between), self.axis, 3)
                self.hop = 1
            elif self.hop == 1:
                self.got.append(self.order.wait(self.flying))
                self.hop = self.n - 1
            return
        if self.direct:
            if self.n > 1:
                got = self.order.wait(*self.flying)
                self.got = [got] if self.n == 2 else list(got)
            self.hop = self.n - 1
            return
        if not self.held:
            self.take()
        self.held = False
        if self.hop < self.n - 1:
            total = self.got[0].astype(F32) + self.blocks[self.hop].astype(F32)
            self.flying = self.order.ring(total.astype(self.between), self.axis)

    def take(self):
        self.got = [self.order.wait(self.flying)]
        self.hop += 1
        self.held = True

    def done(self, parts=0, dtype=BF):
        if self.held:
            self.next()
        while self.hop < self.n - 1:
            self.next()
        terms = [self.blocks[-1]] + (self.got if self.n > 1 else [])

        def total(pick):
            values = [pick(t).astype(F32) for t in terms]
            return functools.reduce(jnp.add, values).astype(dtype)

        if not parts:
            return total(lambda t: t)
        return [total(lambda t, i=i: t[i]) for i in range(parts)]


def behind(place, order_of_axes, value):
    for dim, axis in enumerate(("z", "y", "x")):
        n, at = place.size[axis], place.at[axis]
        picks = [
            lax.dynamic_index_in_dim(value, lax.rem(at - i - 1 + 2 * n, n), dim)
            for i in range(n)
        ]
        value = jnp.concatenate(picks, axis=dim)
    dims = ["zyx".index(axis) for axis in order_of_axes]
    return jnp.transpose(value, tuple(dims) + tuple(range(3, value.ndim)))


def sources(place, order_of_axes, rows):
    lead = tuple(place.size[a] for a in "zyx")
    at = jnp.arange(math.prod(lead) * rows, dtype=jnp.int32).reshape(lead + (rows,))
    return behind(place, order_of_axes, at).reshape(-1)


def compose(earlier, later):
    return jnp.concatenate(
        [earlier[:4] * later[:4], later[:4] * earlier[4:] + later[4:]], axis=0
    )


class Carry:
    def __init__(self, order, end_map, sign, most=3):
        self.order, self.sign, self.most = order, sign, most
        self.n = order.place.seq
        self.unit = jnp.concatenate(
            [jnp.ones_like(end_map[:4]), jnp.zeros_like(end_map[4:])], axis=0
        )
        self.total = None
        self.reach = 0
        self.send(end_map, 1)

    def send(self, value, width):
        self.shifts = []
        distance = max(self.reach, 1)
        while distance < self.n and len(self.shifts) < self.most:
            self.shifts.append(distance)
            distance += width
        self.width = width
        self.flying = [self.order.along(value, self.sign * d) for d in self.shifts]

    def next(self):
        got = self.order.wait(*self.flying)
        got = [got] if len(self.flying) == 1 else list(got)
        s, n = self.order.place.s, self.n
        for value, d in zip(got, self.shifts):
            inside = (s >= d) if self.sign > 0 else (s < n - d)
            part = jnp.where(inside, value, self.unit)
            self.total = part if self.total is None else compose(part, self.total)
        self.reach += self.width * len(self.shifts)
        if self.reach < self.n - 1:
            self.send(self.total, self.reach)
            return True
        return False

    def done(self):
        while self.next():
            pass
        return self.total[4:]


def dot(a, b):
    return jnp.dot(a, b, preferred_element_type=F32)


def dot_nt(a, b):
    return lax.dot_general(a, b, (((1,), (1,)), ((), ())), preferred_element_type=F32)


def dot_tn(a, b):
    return lax.dot_general(a, b, (((0,), (0,)), ((), ())), preferred_element_type=F32)


def moved(value, distance, fill):
    n = value.shape[0]
    size = abs(distance)
    edge = jnp.full((size,) + value.shape[1:], fill, value.dtype)
    if size % 8 == 0:
        if distance > 0:
            return jnp.concatenate([edge, value[: n - size]], axis=0)
        return jnp.concatenate([value[size:], edge], axis=0)
    at = lax.broadcasted_iota(jnp.int32, value.shape, 0)
    turned = pltpu.roll(value, distance % n, 0)
    inside = at >= size if distance > 0 else at < n - size
    return jnp.where(inside, turned, fill)


def scan_tile(decay, drive, sign):
    n = decay.shape[0]
    distance = 1
    while distance < n:
        drive = decay * moved(drive, sign * distance, 0.0) + drive
        decay = decay * moved(decay, sign * distance, 1.0)
        distance *= 2
    return decay, drive


def one_less_exp(u):
    term = jnp.full_like(u, 1.0 / 3628800.0)
    for k in (362880, 40320, 5040, 720, 120, 24, 6, 2):
        term = 1.0 / k - u * term
    small = u * (1.0 - u * term)
    return jnp.where(u < 0.8, small, 1.0 - jnp.exp(-u))


def log2(n):
    return n.bit_length() - 1


def source_rows(order, sizes, at_ref, rows, first, count):
    spot = {"z": at_ref[0], "y": at_ref[1], "x": at_ref[2]}
    size = dict(zip("zyx", sizes))
    line = first + lax.broadcasted_iota(jnp.int32, (count, 1), 0)
    inside = line & (rows - 1)
    line = line >> log2(rows)
    where = {}
    for axis in reversed(order):
        n = size[axis]
        where[axis] = (spot[axis] + (n - 1) - (line & (n - 1))) & (n - 1)
        line = line >> log2(n)
    chip = (where["z"] * size["y"] + where["y"]) * size["x"] + where["x"]
    return chip * rows + inside


def turn_rows(order, sizes, at_ref, value, rows, out_ref):
    total = value.shape[1]
    step = min(total, 256)
    for first in range(0, total, step):
        source = source_rows(order, sizes, at_ref, rows, first, step)
        lane = lax.broadcasted_iota(jnp.int32, (step, total), 1)
        pick = jnp.where(source == lane, 1.0, 0.0).astype(BF)
        out_ref[first : first + step] = dot_nt(pick, value).astype(BF)


def gelu_parts(value):
    square = value * value
    t = jnp.tanh(GELU_C * value * (1.0 + 0.044715 * square))
    half = 0.5 * (1.0 + t)
    slope = half + 0.5 * value * (1.0 - t * t) * GELU_C * (1.0 + 3.0 * 0.044715 * square)
    return value * half, slope


def full(shape):
    return pl.BlockSpec(shape, lambda j: (0,) * len(shape))


def columns(rows, width=TILE):
    return pl.BlockSpec((rows, width), lambda j: (0, j))


def lines(rows, width):
    return pl.BlockSpec((rows, width), lambda j: (j, 0))


def in_hbm(shape, dtype):
    return pltpu.HBM(shape, dtype)


def piece_specs(pieces, rows, tile=TILE):
    if len(pieces) == 1:
        return [columns(pieces[0].shape[0], tile)]
    block = pieces[0].shape[:3] + (rows, tile)
    return [pl.BlockSpec(block, lambda j: (0, 0, 0, 0, j)) for _ in pieces]


def piece_scratch(place, pieces, rows, tile=TILE):
    if len(pieces) == 1:
        return pltpu.VMEM((16, 128), BF)
    return pltpu.VMEM(place.sizes + (rows, tile), BF)


def from_pieces(at, dim, refs, out_ref):
    n = len(refs)
    if n == 1:
        return refs[0][...]
    for k, ref in enumerate(refs):
        where = pl.ds((at - k + n) & (n - 1), 1)
        out_ref[(slice(None),) * dim + (where,)] = ref[...]
    whole = out_ref[...]
    return whole.reshape(-1, whole.shape[-1])


def shape_of(shape, dtype):
    return jax.ShapeDtypeStruct(shape, dtype)


def params(limit):
    return pltpu.CompilerParams(vmem_limit_bytes=limit * MIB)


LIGHT = pl.CostEstimate(flops=1, bytes_accessed=1, transcendentals=0)


def turn_kernel(sizes, rows, at_ref, first_ref, left_ref, right_ref):
    turn_rows("xyz", sizes, at_ref, first_ref[...], rows, left_ref)
    turn_rows("yxz", sizes, at_ref, first_ref[...], rows, right_ref)


def turn_call(place, first, rows):
    length, model = first.shape
    whole = pl.BlockSpec(memory_space=pltpu.VMEM)
    return pl.pallas_call(
        functools.partial(turn_kernel, place.sizes, rows),
        in_specs=[pl.BlockSpec(memory_space=pltpu.SMEM), whole],
        out_specs=[whole] * 2,
        out_shape=[shape_of((model, length), BF)] * 2,
        compiler_params=params(24),
        cost_estimate=LIGHT,
        name="turn",
    )(place.where, first)


def small_kernel(d_rows, r_rows, at_ref, small_ref, qd_ref, md_ref, qr_ref, mr_ref, gain_ref, vec_ref):
    def spread(row, q_ref, m_ref):
        value = dot(small_ref[:, row, :], q_ref[...])
        return jnp.sum(value * m_ref[...], axis=0, keepdims=True)

    for k in range(2):
        gain_ref[k : k + 1] = spread(k, qd_ref, md_ref)
    half = vec_ref.shape[1]
    for k in range(8):
        value = spread(2 + k, qr_ref, mr_ref)
        value = jnp.where(at_ref[3] == 0, value[:, :half], value[:, half:])
        if k == 7:
            soft = jnp.maximum(value, 0.0) + jnp.log1p(jnp.exp(-jnp.abs(value)))
            vec_ref[8:9] = -8.0 * jax.nn.sigmoid(value)
            value = 8.0 * soft
        vec_ref[k : k + 1] = value


def small_call(place, small, d_rows, r_rows):
    devices, _, span = small.shape
    operands = []
    for rows in (d_rows, r_rows):
        lane = np.arange(devices * rows)
        operands.append(jnp.asarray(lane[None] % rows == np.arange(span)[:, None], BF))
        operands.append(jnp.asarray(lane[None] // rows == np.arange(devices)[:, None], F32))
    whole = pl.BlockSpec(memory_space=pltpu.VMEM)
    return pl.pallas_call(
        functools.partial(small_kernel, d_rows, r_rows),
        in_specs=[pl.BlockSpec(memory_space=pltpu.SMEM)] + [whole] * 5,
        out_specs=[whole] * 2,
        out_shape=[shape_of((2, devices * d_rows), F32), shape_of((16, devices * r_rows // 2), F32)],
        compiler_params=params(24),
        cost_estimate=LIGHT,
        name="small_weights",
    )(place.where, small, *operands)


def norm_kernel(n_terms, row, *refs):
    terms, gain_ref, outs = refs[:n_terms], refs[n_terms], refs[n_terms + 1 :]
    value = functools.reduce(jnp.add, [t[...] for t in terms])
    scale = lax.rsqrt(jnp.mean(value * value, axis=-1, keepdims=True) + EPS)
    outs[0][...] = (value * scale * gain_ref[row : row + 1]).astype(BF)
    if n_terms > 1:
        outs[1][...] = value


def norm_call(terms, gains, row):
    tokens, model = terms[0].shape
    step = tokens // 4
    block = pl.BlockSpec((step, model), lambda j: (j, 0))
    shapes = [in_hbm((tokens, model), BF), shape_of((tokens, model), F32)]
    shapes = shapes[: 1 if len(terms) == 1 else 2]
    return pl.pallas_call(
        functools.partial(norm_kernel, len(terms), row),
        grid=(4,),
        in_specs=[block] * len(terms) + [full(gains.shape)],
        out_specs=[block] * len(shapes),
        out_shape=shapes,
        compiler_params=params(16),
        cost_estimate=LIGHT,
        name="norm",
    )(*terms, gains)


def norm_back_kernel(n_terms, row, low, *refs):
    terms = refs[:n_terms]
    value_ref, gain_ref, add_ref, out_ref = refs[n_terms : n_terms + 4]
    gain_out = refs[-1]
    grad = functools.reduce(jnp.add, [t[...] for t in terms])
    value = value_ref[...]
    scale = lax.rsqrt(jnp.mean(value * value, axis=-1, keepdims=True) + EPS)
    unit = value * scale
    inner = grad * gain_ref[row : row + 1]
    total = add_ref[...] + scale * (inner - unit * jnp.mean(inner * unit, axis=-1, keepdims=True))
    out_ref[...] = total
    if low:
        refs[n_terms + 4][...] = total.astype(BF)
    part = jnp.sum(grad * unit, axis=0, keepdims=True)

    @pl.when(pl.program_id(0) == 0)
    def _():
        gain_out[...] = part

    @pl.when(pl.program_id(0) > 0)
    def _():
        gain_out[...] += part


def norm_back_call(terms, value, gains, row, add, low):
    tokens, model = value.shape
    step = tokens // 4
    block = pl.BlockSpec((step, model), lambda j: (j, 0))
    shapes = [shape_of((tokens, model), F32)] + [in_hbm((tokens, model), BF)] * low
    return pl.pallas_call(
        functools.partial(norm_back_kernel, len(terms), row, low),
        grid=(4,),
        in_specs=[block] * len(terms) + [block, full(gains.shape), block],
        out_specs=[block] * len(shapes) + [full((1, model))],
        out_shape=shapes + [shape_of((1, model), F32)],
        compiler_params=params(16),
        cost_estimate=LIGHT,
        name="norm_back",
    )(*terms, value, gains, add)


def pack_kernel(at_ref, go_ref, gr_ref, gi_ref, gvec_ref, vec_ref, mine_ref, other_ref):
    pairs, rows, _ = mine_ref.shape
    model, block = go_ref.shape[1], gr_ref.shape[1]
    line = lax.broadcasted_iota(jnp.int32, gvec_ref.shape, 0)
    gvec = jnp.where(line == 7, gvec_ref[...] * vec_ref[8:9], gvec_ref[...]).astype(BF)
    slot = lax.broadcasted_iota(jnp.int32, (8, block), 0)
    lane = lax.broadcasted_iota(jnp.int32, (8, block), 1)
    turned = dot_tn(gvec, jnp.where(slot == lane, 1.0, 0.0).astype(BF)).astype(BF)
    gr, gi = gr_ref[...].astype(BF), gi_ref[...].astype(BF)
    for k in range(2):

        @pl.when(at_ref[3] == k)
        def _():
            for q in range(pairs):
                for ref, which in ((mine_ref, k), (other_ref, 1 - k)):
                    span = slice((2 * q + which) * rows, (2 * q + which + 1) * rows)
                    ref[q, :, 0:model] = go_ref[span]
                    ref[q, :, model : model + block] = gr[span]
                    ref[q, :, model + block : model + 2 * block] = gi[span]
                    ref[q, :, model + 2 * block :] = turned[span]


def pack_call(place, g_out, g_gate_r, g_gate_i, g_vec, vec, rows):
    width, model = g_out.shape
    block = g_gate_r.shape[1]
    shape = (width // (2 * rows), rows, model + 3 * block)
    whole = pl.BlockSpec(memory_space=pltpu.VMEM)
    return pl.pallas_call(
        pack_kernel,
        in_specs=[pl.BlockSpec(memory_space=pltpu.SMEM)] + [whole] * 5,
        out_specs=[whole] * 2,
        out_shape=[shape_of(shape, BF), shape_of(shape, BF)],
        compiler_params=params(24),
        cost_estimate=LIGHT,
        name="pack",
    )(place.where, g_out, g_gate_r, g_gate_i, g_vec, vec)


def forward_kernel(
    n_rows,
    group,
    block,
    n_in,
    n_branch,
    at_ref,
    mine_ref,
    other_ref,
    halo_ref,
    *refs,
):
    w_refs, wb_refs, refs = refs[:n_in], refs[n_in : n_in + n_branch], refs[n_in + n_branch :]
    vec_ref, mask_ref, gr_ref, gi_ref, first_ref, bpre_ref, mixer_ref, conv_ref = refs[:8]
    rpre_ref, ipre_ref, through_ref, local_ref, ends_ref, w_ref, wb_ref = refs[8:15]
    ext_ref, in_ref, branch_ref = refs[15:]
    half = mine_ref.shape[0]
    w_ref[...] = from_pieces(at_ref[2], 2, w_refs, in_ref)
    wb_ref[...] = from_pieces(at_ref[1], 1, wb_refs, branch_ref)

    @pl.when(pl.program_id(0) == 0)
    def _():
        first_ref[0:half] = mine_ref[...]
        first_ref[half : 2 * half] = other_ref[...]
        first_ref[2 * half :] = halo_ref[...]

    mixer = dot(first_ref[...], w_ref[...]).astype(BF)
    bpre_ref[...] = dot(first_ref[0 : 2 * half], wb_ref[...])
    mixer_ref[...] = mixer
    wide = mixer.astype(F32)
    tokens = n_rows * group
    for r in range(n_rows):
        ext_ref[r, 0:HALO] = wide[tokens + HALO * r : tokens + HALO * (r + 1)]
        ext_ref[r, HALO : HALO + group] = wide[r * group : (r + 1) * group]
    for r in range(n_rows):
        span = slice(r * group, (r + 1) * group)
        conv = vec_ref[4:5] + vec_ref[0:1] * ext_ref[r, HALO : HALO + group]
        for k in range(1, 4):
            conv += (
                vec_ref[k : k + 1]
                * ext_ref[r, HALO - k : HALO - k + group]
                * mask_ref[span, k : k + 1]
            )
        conv_ref[span] = conv.astype(BF)
    for h in range(w_ref.shape[1] // block):
        cols = slice(h * block, (h + 1) * block)
        low = conv_ref[:, cols]
        rpre_ref[:, cols] = dot(low, gr_ref[cols]) + vec_ref[5:6, cols]
        ipre_ref[:, cols] = dot(low, gi_ref[cols]) + vec_ref[6:7, cols]
        for r in range(n_rows):
            span = slice(r * group, (r + 1) * group)
            recur = jax.nn.sigmoid(rpre_ref[span, cols])
            admit = jax.nn.sigmoid(ipre_ref[span, cols])
            rate = vec_ref[7:8, cols] * recur
            reset = mask_ref[span, 0:1]
            decay = jnp.exp(-rate) * (1.0 - reset)
            scale = jnp.where(reset > 0.5, 1.0, jnp.sqrt(one_less_exp(2.0 * rate)))
            drive = scale * admit * conv_ref[span, cols].astype(F32)
            decay, drive = scan_tile(decay, drive, 1)
            through_ref[span, cols] = decay
            local_ref[span, cols] = drive
            ends_ref[r : r + 1, cols] = decay[group - 1 : group]
            ends_ref[n_rows + r : n_rows + r + 1, cols] = drive[group - 1 : group]


def forward_call(place, mine, other, halo, w_in, w_branch, vec, masks, gate_r, gate_i, n_rows, group, chip_d):
    model = mine.shape[1]
    length = 2 * mine.shape[0] + halo.shape[0]
    width, block = w_in[0].shape[-1], gate_r.shape[1]
    tokens = n_rows * group
    tile = TILE
    return pl.pallas_call(
        functools.partial(
            forward_kernel, n_rows, group, block, len(w_in), len(w_branch)
        ),
        grid=(width // tile,),
        in_specs=[
            pl.BlockSpec(memory_space=pltpu.SMEM),
            full(mine.shape),
            full(mine.shape),
            full(halo.shape),
            *piece_specs(w_in, chip_d),
            *piece_specs(w_branch, chip_d),
            columns(16),
            full(masks.shape),
            lines(tile, block),
            lines(tile, block),
        ],
        out_specs=[full((length, model)), columns(tokens), columns(length)]
        + [columns(tokens)] * 5
        + [columns(2 * n_rows), columns(model), columns(model)],
        out_shape=[
            in_hbm((length, model), BF),
            in_hbm((tokens, width), F32),
            in_hbm((length, width), BF),
            in_hbm((tokens, width), BF),
            in_hbm((tokens, width), F32),
            in_hbm((tokens, width), F32),
            in_hbm((tokens, width), F32),
            in_hbm((tokens, width), F32),
            in_hbm((2 * n_rows, width), F32),
            in_hbm((model, width), BF),
            in_hbm((model, width), BF),
        ],
        scratch_shapes=[
            pltpu.VMEM((n_rows, HALO + group, tile), F32),
            piece_scratch(place, w_in, chip_d),
            piece_scratch(place, w_branch, chip_d),
        ],
        compiler_params=params(24),
        cost_estimate=LIGHT,
        name="recurrence_forward",
    )(place.where, mine, other, halo, *w_in, *w_branch, vec, masks, gate_r, gate_i)


def mix_kernel(
    n_rows, group, local_ref, through_ref, enter_ref, bpre_ref, w_ref, state_ref, mixed_ref, part_ref, part_other_ref
):
    for r in range(n_rows):
        span = slice(r * group, (r + 1) * group)
        state = local_ref[span] + through_ref[span] * enter_ref[r : r + 1]
        state_ref[span] = state
        branch, _ = gelu_parts(bpre_ref[span])
        mixed_ref[span] = (state * branch).astype(BF)
    part = dot(mixed_ref[...], w_ref[...])
    half = part_ref.shape[0]

    @pl.when(pl.program_id(0) == 0)
    def _():
        part_ref[...] = part[:half]
        part_other_ref[...] = part[half:]

    @pl.when(pl.program_id(0) > 0)
    def _():
        part_ref[...] += part[:half]
        part_other_ref[...] += part[half:]


def mix_call(local, through, enter, branch_pre, w_out, n_rows, group):
    tokens, width = local.shape
    model = w_out.shape[1]
    return pl.pallas_call(
        functools.partial(mix_kernel, n_rows, group),
        grid=(width // TILE,),
        in_specs=[
            columns(tokens),
            columns(tokens),
            columns(n_rows),
            columns(tokens),
            lines(TILE, model),
        ],
        out_specs=[columns(tokens), columns(tokens)] + [full((tokens // 2, model))] * 2,
        out_shape=[
            in_hbm((tokens, width), F32),
            in_hbm((tokens, width), BF),
            shape_of((tokens // 2, model), F32),
            in_hbm((tokens // 2, model), F32),
        ],
        compiler_params=params(58),
        cost_estimate=LIGHT,
        name="mix",
    )(local, through, enter, branch_pre, w_out)


def ffn_kernel(
    sizes,
    rows,
    n_gate,
    n_up,
    at_ref,
    mine_ref,
    other_ref,
    low_mine_ref,
    low_other_ref,
    *refs,
):
    wg_refs, wu_refs, refs = refs[:n_gate], refs[n_gate : n_gate + n_up], refs[n_gate + n_up :]
    wd_ref, gg_send_ref, gg_ref, gu_send_ref, gu_ref, gd_ref, gd_other_ref = refs[:7]
    part_ref, part_other_ref, back_ref, back_other_ref = refs[7:11]
    second_ref, low_ref, left_ref, right_ref, gate_ref, up_ref, down_ref = refs[11:]
    step = pl.program_id(0)
    half = mine_ref.shape[0]

    @pl.when(step == 0)
    def _():
        second_ref[0:half] = mine_ref[...]
        second_ref[half:] = other_ref[...]
        low_ref[0:half] = low_mine_ref[...]
        low_ref[half:] = low_other_ref[...]
        turn_rows("xyz", sizes, at_ref, second_ref[...], rows, left_ref)
        turn_rows("yxz", sizes, at_ref, second_ref[...], rows, right_ref)

    second, low = second_ref[...], low_ref[...]
    w_gate = from_pieces(at_ref[2], 2, wg_refs, gate_ref)
    w_up = from_pieces(at_ref[1], 1, wu_refs, up_ref)
    gate = dot(second, w_gate)
    up = dot(second, w_up)
    grad = dot_nt(low, wd_ref[...])
    active, slope = gelu_parts(gate)
    hidden = (active * up).astype(BF)
    gate_low = (grad * up * slope).astype(BF)
    up_low = (grad * active).astype(BF)
    sent = gg_send_ref.shape[0]
    gg = dot(left_ref[...], gate_low).astype(BF)
    gg_send_ref[...] = gg[:sent]
    gg_ref[...] = gg[sent:]
    sent = gu_send_ref.shape[0]
    gu = dot(right_ref[...], up_low).astype(BF)
    gu_send_ref[...] = gu[:sent]
    gu_ref[...] = gu[sent:]
    width = hidden.shape[1]
    down_ref[pl.ds(step * width, width)] = dot_tn(hidden, low).astype(BF)
    part = dot(hidden, wd_ref[...])
    back = dot_nt(gate_low, w_gate) + dot_nt(up_low, w_up)

    @pl.when(step == 0)
    def _():
        part_ref[...] = part[:half]
        part_other_ref[...] = part[half:]
        back_ref[...] = back[:half]
        back_other_ref[...] = back[half:]

    @pl.when(step > 0)
    def _():
        part_ref[...] += part[:half]
        part_other_ref[...] += part[half:]
        back_ref[...] += back[:half]
        back_other_ref[...] += back[half:]

    pairs, lines_down, _ = gd_ref.shape
    for k in range(2):

        @pl.when((step == pl.num_programs(0) - 1) & (at_ref[3] == k))
        def _():
            for q in range(pairs):
                at = 2 * q * lines_down
                near, far = at + k * lines_down, at + (1 - k) * lines_down
                gd_ref[q] = down_ref[near : near + lines_down]
                gd_other_ref[q] = down_ref[far : far + lines_down]


def ffn_call(place, mine, other, low_mine, low_other, w_gate, w_up, w_down, chip_d, f_rows):
    tokens, model = 2 * mine.shape[0], mine.shape[1]
    width = w_gate[0].shape[-1]
    tile = 2 * TILE
    sent_l, sent_r = model // place.size["x"], model // place.size["y"]
    down = (width // (2 * f_rows), f_rows, model)
    rows = [sent_l, model - sent_l, sent_r, model - sent_r]
    return pl.pallas_call(
        functools.partial(ffn_kernel, place.sizes, chip_d, len(w_gate), len(w_up)),
        grid=(width // tile,),
        in_specs=[
            pl.BlockSpec(memory_space=pltpu.SMEM),
            full((tokens // 2, model)),
            full((tokens // 2, model)),
            full((tokens // 2, model)),
            full((tokens // 2, model)),
            *piece_specs(w_gate, chip_d, tile),
            *piece_specs(w_up, chip_d, tile),
            lines(tile, model),
        ],
        out_specs=[columns(n, tile) for n in rows]
        + [full(down)] * 2
        + [full((tokens // 2, model))] * 4,
        out_shape=[in_hbm((n, width), BF) for n in rows]
        + [shape_of(down, BF), in_hbm(down, BF)]
        + [shape_of((tokens // 2, model), F32), in_hbm((tokens // 2, model), F32)] * 2,
        scratch_shapes=[
            pltpu.VMEM((tokens, model), BF),
            pltpu.VMEM((tokens, model), BF),
            pltpu.VMEM((model, tokens), BF),
            pltpu.VMEM((model, tokens), BF),
            piece_scratch(place, w_gate, chip_d, tile),
            piece_scratch(place, w_up, chip_d, tile),
            pltpu.VMEM((width, model), BF),
        ],
        compiler_params=params(60),
        cost_estimate=LIGHT,
        name="feed_forward",
    )(place.where, mine, other, low_mine, low_other, *w_gate, *w_up, w_down)


def split_kernel(cuts, at_ref, whole_ref, *outs):
    for out, (low, high) in zip(outs, cuts):
        out[...] = whole_ref[:, low:high]


def split_call(place, whole, cuts):
    count, rows, width = whole.shape
    steps = 4
    step = count // (2 * steps)
    if any(n % 16 for cut in cuts for n in cut):
        half = lax.dynamic_slice_in_dim(whole, place.at["c"] * (count // 2), count // 2, 0)
        return [half[:, low:high].reshape(-1, width) for low, high in cuts]
    outs = pl.pallas_call(
        functools.partial(split_kernel, cuts),
        grid_spec=pltpu.PrefetchScalarGridSpec(
            num_scalar_prefetch=1,
            grid=(steps,),
            in_specs=[pl.BlockSpec((step, rows, width), lambda j, at: (at[3] * steps + j, 0, 0))],
            out_specs=[
                pl.BlockSpec((step, high - low, width), lambda j, at: (j, 0, 0))
                for low, high in cuts
            ],
        ),
        out_shape=[in_hbm((count // 2, high - low, width), BF) for low, high in cuts],
        compiler_params=params(58),
        cost_estimate=LIGHT,
        name="split",
    )(place.where, whole)
    return [out.reshape(-1, width) for out in outs]


def regroup_kernel(sizes, order_of, cuts, at_ref, mine_ref, got_ref, *outs):
    nz, ny, nx = sizes
    size = {"z": nz, "y": ny, "x": nx}
    spot = {"z": at_ref[0], "y": at_ref[1], "x": at_ref[2]}
    half = mine_ref.shape[0]
    for index, order in enumerate(order_of):
        send_ref, rest_ref = outs[2 * index], outs[2 * index + 1]
        span = slice(*cuts[index])
        for i0 in range(size[order[0]]):
            for i1 in range(size[order[1]]):
                for i2 in range(size[order[2]]):
                    place = {}
                    for axis, i in zip(order, (i0, i1, i2)):
                        n = size[axis]
                        place[axis] = lax.rem(spot[axis] + (n - 1 - i), n)
                    chip = (place["z"] * ny + place["y"]) * nx + place["x"]
                    here = lax.rem(chip, half)
                    own = lax.div(chip, half) == at_ref[3]
                    value = jnp.where(own, mine_ref[here][:, span], got_ref[here][:, span])
                    if i0 == 0:
                        send_ref[i1, i2] = value
                    else:
                        rest_ref[i0 - 1, i1, i2] = value


def regroup_call(place, mine, got, order_of, cuts):
    sizes = tuple(place.size[a] for a in "zyx")
    rows = mine.shape[1]
    shapes = []
    for order, (low, high) in zip(order_of, cuts):
        n0, n1, n2 = (place.size[a] for a in order)
        shapes.append((n1, n2, rows, high - low))
        shapes.append((n0 - 1, n1, n2, rows, high - low))
    whole = pl.BlockSpec(memory_space=pltpu.VMEM)
    outs = pl.pallas_call(
        functools.partial(regroup_kernel, sizes, order_of, cuts),
        in_specs=[pl.BlockSpec(memory_space=pltpu.SMEM), whole, whole],
        out_specs=[whole] * len(shapes),
        out_shape=[shape_of(shape, BF) for shape in shapes],
        compiler_params=params(24),
        cost_estimate=LIGHT,
        name="regroup",
    )(place.where, mine, got)
    return [
        [outs[2 * i]] + [outs[2 * i + 1][j] for j in range(shapes[2 * i + 1][0])]
        for i in range(len(order_of))
    ]


def decay_of(rpre, vec7, reset):
    recur = jax.nn.sigmoid(rpre)
    rate = vec7 * recur
    return recur, rate, jnp.exp(-rate) * (1.0 - reset)


def back_kernel(
    n_rows,
    group,
    mine_ref,
    other_ref,
    w_ref,
    bpre_ref,
    state_ref,
    rpre_ref,
    mixed_ref,
    vec_ref,
    mask_ref,
    right_ref,
    go_ref,
    gb_send_ref,
    gb_ref,
    gbl_ref,
    reach_ref,
    local_ref,
    ends_ref,
    low_ref,
    grad_ref,
):
    @pl.when(pl.program_id(0) == 0)
    def _():
        half = mine_ref.shape[0]
        low_ref[0:half] = mine_ref[...]
        low_ref[half:] = other_ref[...]

    low = low_ref[...]
    grad_ref[...] = dot_nt(low, w_ref[...])
    go_ref[...] = dot_tn(mixed_ref[...], low).astype(BF)
    half = w_ref.shape[0] // 2
    for h in range(2):
        cols = slice(h * half, (h + 1) * half)
        for r in range(n_rows):
            span = slice(r * group, (r + 1) * group)
            branch, slope = gelu_parts(bpre_ref[span, cols])
            grad = grad_ref[span, cols]
            gbl_ref[span, cols] = (grad * state_ref[span, cols] * slope).astype(BF)
            _, _, decay = decay_of(rpre_ref[span, cols], vec_ref[7:8, cols], mask_ref[span, 0:1])
            ahead = moved(decay, -1, 1.0)
            reach, local = scan_tile(ahead, grad * branch, -1)
            reach_ref[span, cols] = reach
            local_ref[span, cols] = local
            ends_ref[r : r + 1, cols] = decay[0:1] * reach[0:1]
            ends_ref[n_rows + r : n_rows + r + 1, cols] = decay[0:1] * local[0:1]
    sent = gb_send_ref.shape[0]
    gb = dot(right_ref[:, 0 : gbl_ref.shape[0]], gbl_ref[...]).astype(BF)
    gb_send_ref[...] = gb[:sent]
    gb_ref[...] = gb[sent:]


def back_call(place, mine, other, w_out, branch_pre, state, rpre, mixed, vec, masks, right, n_rows, group):
    model, length = right.shape
    tokens = state.shape[0]
    sent = model // place.size["y"]
    width = w_out.shape[0]
    return pl.pallas_call(
        functools.partial(back_kernel, n_rows, group),
        grid=(width // TILE,),
        in_specs=[
            full((tokens // 2, model)),
            full((tokens // 2, model)),
            lines(TILE, model),
            columns(tokens),
            columns(tokens),
            columns(tokens),
            columns(tokens),
            columns(16),
            full(masks.shape),
            full((model, length)),
        ],
        out_specs=[
            lines(TILE, model),
            columns(sent),
            columns(model - sent),
            columns(tokens),
            columns(tokens),
            columns(tokens),
            columns(2 * n_rows),
        ],
        out_shape=[
            shape_of((width, model), BF),
            in_hbm((sent, width), BF),
            in_hbm((model - sent, width), BF),
            shape_of((tokens, width), BF),
            shape_of((tokens, width), F32),
            shape_of((tokens, width), F32),
            shape_of((2 * n_rows, width), F32),
        ],
        scratch_shapes=[pltpu.VMEM((tokens, model), BF), pltpu.VMEM((tokens, TILE), F32)],
        compiler_params=params(32),
        cost_estimate=LIGHT,
        name="recurrence_back",
    )(mine, other, w_out, branch_pre, state, rpre, mixed, vec, masks, right)


def gates_kernel(
    n_rows,
    group,
    block,
    reach_ref,
    local_ref,
    leave_ref,
    state_ref,
    enter_ref,
    rpre_ref,
    ipre_ref,
    conv_ref,
    mixer_ref,
    vec_ref,
    mask_ref,
    gr_ref,
    gi_ref,
    left_ref,
    win_ref,
    wbr_ref,
    gbl_ref,
    gin_send_ref,
    gin_ref,
    ggr_ref,
    ggi_ref,
    gvec_ref,
    gfirst_ref,
    rlow_ref,
    ilow_ref,
    gconv_ref,
    ext_ref,
    spread_ref,
    gm_ref,
):
    step = pl.program_id(0)
    tokens = n_rows * group

    gvec_ref[...] = jnp.zeros_like(gvec_ref)
    for h in range(win_ref.shape[1] // block):
        cols = slice(h * block, (h + 1) * block)
        for r in range(n_rows):
            span = slice(r * group, (r + 1) * group)
            adjoint = local_ref[span, cols] + reach_ref[span, cols] * leave_ref[r : r + 1, cols]
            state = state_ref[span, cols]
            at = lax.broadcasted_iota(jnp.int32, state.shape, 0)
            before = jnp.where(at == 0, enter_ref[r : r + 1, cols], pltpu.roll(state, 1, 0))
            reset = mask_ref[span, 0:1]
            live = 1.0 - reset
            recur, rate, decay = decay_of(rpre_ref[span, cols], vec_ref[7:8, cols], reset)
            admit = jax.nn.sigmoid(ipre_ref[span, cols])
            full_decay = jnp.exp(-rate)
            root = jnp.sqrt(one_less_exp(2.0 * rate))
            scale = jnp.where(reset > 0.5, 1.0, root)
            conv = conv_ref[span, cols].astype(F32)
            direct = adjoint * scale
            gadmit = direct * conv
            gconv_ref[span, cols] = direct * admit
            gscale = adjoint * admit * conv
            glog = live * full_decay * (adjoint * before - gscale * full_decay / root)
            gvec_ref[7:8, cols] += jnp.sum(glog * recur, axis=0, keepdims=True)
            grecur = -(vec_ref[7:8, cols] * glog) * recur * (1.0 - recur)
            ginput = gadmit * admit * (1.0 - admit)
            rlow, ilow = grecur.astype(BF), ginput.astype(BF)
            rlow_ref[span, cols] = rlow
            ilow_ref[span, cols] = ilow
            gvec_ref[5:6, cols] += jnp.sum(rlow.astype(F32), axis=0, keepdims=True)
            gvec_ref[6:7, cols] += jnp.sum(ilow.astype(F32), axis=0, keepdims=True)
        rlow, ilow = rlow_ref[:, cols], ilow_ref[:, cols]
        low = conv_ref[:, cols]
        ggr_ref[cols] = dot_tn(low, rlow)
        ggi_ref[cols] = dot_tn(low, ilow)
        gconv_ref[:, cols] += dot_nt(rlow, gr_ref[cols]) + dot_nt(ilow, gi_ref[cols])
        for r in range(n_rows):
            span = slice(r * group, (r + 1) * group)
            head = slice(tokens + HALO * r, tokens + HALO * (r + 1))
            ext_ref[0:HALO] = mixer_ref[head, cols].astype(F32)
            ext_ref[HALO : HALO + group] = mixer_ref[span, cols].astype(F32)
            gconv = gconv_ref[span, cols]
            gvec_ref[4:5, cols] += jnp.sum(gconv, axis=0, keepdims=True)
            gvec_ref[0:1, cols] += jnp.sum(
                gconv * ext_ref[HALO : HALO + group], axis=0, keepdims=True
            )
            spread_ref[0:HALO] = jnp.zeros((HALO, block), F32)
            spread_ref[HALO : HALO + group] = vec_ref[0:1, cols] * gconv
            for k in range(1, 4):
                masked = gconv * mask_ref[span, k : k + 1]
                there = slice(HALO - k, HALO - k + group)
                gvec_ref[k : k + 1, cols] += jnp.sum(
                    masked * ext_ref[there], axis=0, keepdims=True
                )
                spread_ref[there] += vec_ref[k : k + 1, cols] * masked
            gm_ref[head, cols] = spread_ref[0:HALO].astype(BF)
            gm_ref[span, cols] = spread_ref[HALO : HALO + group].astype(BF)
    gm = gm_ref[...]
    sent = gin_send_ref.shape[0]
    gin = dot(left_ref[...], gm).astype(BF)
    gin_send_ref[...] = gin[:sent]
    gin_ref[...] = gin[sent:]
    part = dot_nt(gm, win_ref[...])
    part_branch = dot_nt(gbl_ref[...], wbr_ref[...])

    @pl.when(step == 0)
    def _():
        gfirst_ref[...] = part

    @pl.when(step > 0)
    def _():
        gfirst_ref[...] += part

    gfirst_ref[0:tokens] += part_branch


def gates_call(
    place, reach, local, leave, state, enter, rpre, ipre, conv, mixer, vec, masks, gate_r, gate_i, left, w_in, w_branch, gbl, n_rows, group
):
    model, length = left.shape
    sent = model // place.size["x"]
    tokens, width = state.shape
    block = gate_r.shape[1]
    tile = TILE
    return pl.pallas_call(
        functools.partial(gates_kernel, n_rows, group, block),
        grid=(width // tile,),
        in_specs=[
            columns(tokens),
            columns(tokens),
            columns(n_rows),
            columns(tokens),
            columns(n_rows),
            columns(tokens),
            columns(tokens),
            columns(tokens),
            columns(length),
            columns(16),
            full(masks.shape),
            lines(tile, block),
            lines(tile, block),
            full((model, length)),
            columns(model),
            columns(model),
            columns(tokens),
        ],
        out_specs=[
            columns(sent),
            columns(model - sent),
            lines(tile, block),
            lines(tile, block),
            columns(8),
            full((length, model)),
        ],
        out_shape=[
            in_hbm((sent, width), BF),
            in_hbm((model - sent, width), BF),
            shape_of((width, block), F32),
            shape_of((width, block), F32),
            shape_of((8, width), F32),
            shape_of((length, model), F32),
        ],
        scratch_shapes=[
            pltpu.VMEM((tokens, tile), BF),
            pltpu.VMEM((tokens, tile), BF),
            pltpu.VMEM((tokens, tile), F32),
            pltpu.VMEM((HALO + group, block), F32),
            pltpu.VMEM((HALO + group, block), F32),
            pltpu.VMEM((length, tile), BF),
        ],
        compiler_params=params(40),
        cost_estimate=LIGHT,
        name="recurrence_gates",
    )(reach, local, leave, state, enter, rpre, ipre, conv, mixer, vec, masks, gate_r, gate_i, left, w_in, w_branch, gbl)


def normed(values, gain):
    return values * lax.rsqrt(jnp.mean(values * values, axis=-1, keepdims=True) + EPS) * gain


def halves(value, place, dim):
    half = value.shape[dim] // 2
    mine = lax.dynamic_slice_in_dim(value, place.at["c"] * half, half, dim)
    other = lax.dynamic_slice_in_dim(value, (1 - place.at["c"]) * half, half, dim)
    return mine, other


def own_channels(place, value):
    mine, other = halves(value, place, 0)
    got = place.ring(other, "c", 1)
    pair = place.ordered(mine, got)
    both = jnp.stack(pair, axis=1)
    return both.reshape(-1, both.shape[-1])


def own_devices(place, value, rows):
    shaped = value.reshape(place.chips // 2, 2, rows, value.shape[-1])
    mine = lax.dynamic_index_in_dim(shaped, place.at["c"], 1, keepdims=False)
    other = lax.dynamic_index_in_dim(shaped, 1 - place.at["c"], 1, keepdims=False)
    got = place.ring(other, "c", 1)
    return jnp.concatenate(place.ordered(mine, got), axis=0)


def on_device(
    inputs,
    cotangent,
    segments,
    norm1_gain,
    input_proj,
    branch_proj,
    conv_weight,
    conv_bias,
    recur_gate,
    input_gate,
    recur_bias,
    input_bias,
    decay_param,
    output_proj,
    norm2_gain,
    mlp_gate,
    mlp_up,
    mlp_down,
):
    place = Place()
    core = place.at["c"]
    chips = place.chips
    rows_dev, group, model = inputs.shape
    n_rows = 2 * rows_dev
    tokens_dev = rows_dev * group
    tokens = 2 * tokens_dev
    d_rows, lru = input_proj.shape
    ffn = mlp_gate.shape[1]
    r_rows, block = recur_gate.shape
    f_rows = mlp_down.shape[0]
    lru_half, ffn_half = lru // 2, ffn // 2
    pair = lambda value: place.ring(value, "c", 1)

    order = Order(place)
    lead = (place.size["z"], place.size["y"], place.size["x"])

    wide = [halves(w, place, 1) for w in (input_proj, branch_proj, mlp_gate, mlp_up)]
    got_a = order.ring(jnp.concatenate([w[1] for w in wide[:2]], axis=1), "c")
    got_c = order.ring(jnp.concatenate([w[1] for w in wide[2:]], axis=1), "c")
    span = max(d_rows, r_rows)
    lines_one = [
        jnp.pad(v, (0, span - v.shape[0]))[None]
        for v in (norm1_gain, norm2_gain, conv_bias, recur_bias, input_bias, decay_param)
    ]
    taps = jnp.pad(conv_weight, ((0, 0), (0, span - r_rows)))
    vectors = jnp.concatenate(lines_one[:2] + [taps] + lines_one[2:], axis=0)
    small = Gather(order, vectors[None, None, None, None], "y", 1)
    ids_pair = order.ring(segments, "c")
    mine_a = jnp.concatenate([w[0] for w in wide[:2]], axis=1)
    mine_c = jnp.concatenate([w[0] for w in wide[2:]], axis=1)
    gates = jnp.concatenate([recur_gate, input_gate], axis=0)
    gate_lines = 2 * r_rows * block // lru
    gates = gates.reshape(-1, gate_lines, block).transpose(1, 0, 2).reshape(gate_lines, lru)
    order.must(gates, mine_a)
    small = Gather(order, small.done(), "x", 2)
    got_a = order.wait(got_a)
    rows_a = jnp.concatenate(place.ordered(mine_a, got_a), axis=0)
    group_a = jnp.concatenate([rows_a, gates], axis=0)[None, None, None]
    order.must(group_a)
    both_whole = jnp.concatenate([output_proj, mlp_down], axis=0)
    both_whole = lax.all_gather(both_whole, AXES, axis=0)
    small = Gather(order, small.done(), "c", 3)
    small = Gather(order, small.done(), "z", 0, direct=True)

    a_z = Gather(order, group_a, "z", 0, direct=True)
    grad_out = cotangent.reshape(tokens_dev, model)
    low = grad_out.astype(BF)
    low_other = order.ring(low, "c")
    ids_pair, got_c = order.wait(ids_pair, got_c)
    ids = jnp.concatenate([segments, ids_pair], axis=0)
    prior_ids = order.along(ids[:, group - 3 :], 1)
    gains, vec = small_call(
        place, small.done().reshape(2 * chips, -1, span), d_rows, r_rows
    )
    flat = inputs.reshape(tokens_dev, model)
    (first,) = norm_call([flat], gains, 0)
    first_other = order.ring(first, "c")
    group_c = jnp.concatenate(place.ordered(mine_c, got_c), axis=0)[None, None, None]
    first_other, low_other = order.wait(first_other, low_other)
    tail = jnp.concatenate(
        [v.reshape(rows_dev, group, model)[:, group - 3 :] for v in (first, first_other)], axis=0
    )
    halo = order.along(tail, 1)
    c_z = Gather(order, group_c, "z", 0, both=True)
    a_z = a_z.done()
    halo, prior_ids = order.wait(halo, prior_ids)

    a_left = Gather(order, a_z[..., :lru_half], "y", 1)
    a_right = Gather(order, a_z[..., lru_half:], "x", 2)
    a_left, a_right = a_left.done(), a_right.done()

    a_left = Gather(order, a_left, "x", 2)
    a_right = Gather(order, a_right, "y", 1)
    c_z.next()
    a_left.arrived()
    a_right.arrived()

    chip_d = 2 * d_rows
    packed = [g.whole([p[..., chip_d:, :] for p in g.pieces]) for g in (a_left, a_right)]
    packed = jnp.concatenate(packed, axis=-1)
    packed = packed.reshape(chips, gate_lines, -1, block)
    packed = packed.transpose(0, 2, 1, 3).reshape(chips, 2, r_rows, block)
    packed = jnp.concatenate([packed[:, 0], packed[:, 1]], axis=-1)
    gate_mine, gate_other = halves(packed, place, 0)
    gate_got = order.ring(gate_other, "c")
    c_z = c_z.done()
    c_left = Gather(order, c_z[..., :ffn_half], "y", 1)
    c_right = Gather(order, c_z[..., ffn_half:], "x", 2)
    halo = jnp.pad(halo, ((0, 0), (HALO - 3, 0), (0, 0))).reshape(n_rows * HALO, model)
    position = place.s * group + jnp.arange(group, dtype=jnp.int32)
    joined_ids = jnp.concatenate([prior_ids, ids], axis=1)
    marks = [(joined_ids[:, 2 : 2 + group] != ids) | (position == 0)[None, :]]
    for k in range(1, 4):
        marks.append(
            (joined_ids[:, 3 - k : 3 - k + group] == ids) & (position >= k)[None, :]
        )
    masks = jnp.stack(marks, axis=-1).astype(F32).reshape(tokens, 4)
    masks = jnp.pad(masks, ((0, 0), (0, 4)))
    gate_got = order.wait(gate_got)
    packed = jnp.stack(place.ordered(gate_mine, gate_got), axis=1).reshape(-1, 2 * block)
    gate_r, gate_i = packed[:, :block], packed[:, block:]
    first_ext, branch_pre, mixer, conv, rpre, ipre, through, local, ends, w_in, w_branch = forward_call(
        place, first, first_other, halo, a_left.weight(chip_d), a_right.weight(chip_d), vec, masks, gate_r, gate_i, n_rows, group, chip_d
    )
    enter = Carry(order, ends, 1)
    more = enter.next()
    c_left, c_right = c_left.done(), c_right.done()

    c_left = Gather(order, c_left, "x", 2)
    c_right = Gather(order, c_right, "y", 1)
    both_whole = order.wait(both_whole)
    w_out, w_down = split_call(
        place, both_whole, ((0, r_rows), (r_rows, r_rows + f_rows))
    )
    order.must(w_out, w_down)
    enter = enter.done() if more else enter.total[4:]
    state, mixed, part, part_other = mix_call(
        local, through, enter, branch_pre, w_out, n_rows, group
    )
    part_pair = order.ring(part_other, "c")
    first_l, first_r = turn_call(place, order.tie(first_ext), chip_d)
    order.must(first_l, first_r)
    w_gate, w_up = c_left.weight(chip_d), c_right.weight(chip_d)
    part_pair = order.wait(part_pair)
    second, middle = norm_call([flat, part, part_pair], gains, 1)
    second_other = order.ring(second, "c")
    second_other = order.wait(second_other)

    nz, ny, nx = lead

    def blocks_of(send, rest, axis, other):
        shape = (place.size[other], nz, chip_d, -1)
        rest = rest.reshape((place.size[axis] - 1,) + shape)
        return [send.reshape(shape)] + [rest[i] for i in range(rest.shape[0])]

    def joined(left, right):
        return [jnp.concatenate(p, axis=-1) for p in zip(left.done(nz), right.done(nz))]

    g_send, g_rest, u_send, u_rest, down_mine, down_other, part, part_other, back, back_other = ffn_call(
        place, second, second_other, low, low_other, w_gate, w_up, w_down, chip_d, f_rows
    )

    back_pair = order.ring(back_other, "c")
    g_left = Scatter(order, blocks_of(g_send, g_rest, "x", "y"), "x")
    g_right = Scatter(order, blocks_of(u_send, u_rest, "y", "x"), "y")
    down_got = order.ring(down_other, "c")
    back_pair = order.wait(back_pair)
    grad_middle, mid_low, grad_gain_two = norm_back_call(
        [back, back_pair], middle, gains, 1, grad_out, 1
    )
    mid_pair = order.ring(mid_low, "c")
    down_got = order.wait(down_got)
    (d_z,) = regroup_call(place, down_mine, down_got, ("zyx",), ((0, model),))
    d_z = Scatter(order, d_z, "z")
    mid_other = order.wait(mid_pair)
    g_out, b_send, b_rest, gbl, reach, local_back, ends_back = back_call(
        place, mid_low, mid_other, w_out, branch_pre, state, rpre, mixed, vec, masks, first_r, n_rows, group
    )
    d_z.take()
    leave = Carry(order, ends_back, -1)
    g_left.next()
    g_right.next()
    more = leave.next()

    g_left = Scatter(order, g_left.done(ny), "y")
    g_right = Scatter(order, g_right.done(nx), "x")
    leave = leave.done() if more else leave.total[4:]
    d_z.next()
    in_send, in_rest, g_gate_r, g_gate_i, g_vec, grad_first = gates_call(
        place, reach, local_back, leave, state, enter, rpre, ipre, conv, mixer, vec, masks, gate_r, gate_i, first_l, w_in, w_branch, gbl, n_rows, group
    )
    order.must(in_send)
    g_left.next()
    g_right.next()
    d_z.take()

    a_left = Scatter(order, blocks_of(in_send, in_rest, "x", "y"), "x")
    a_right = Scatter(order, blocks_of(b_send, b_rest, "y", "x"), "y")
    out_mine, out_other = pack_call(place, g_out, g_gate_r, g_gate_i, g_vec, vec, r_rows)
    out_got = order.ring(out_other, "c")
    out_got = order.wait(out_got)
    wide_r = out_mine.shape[-1]
    cut = (wide_r // (2 * block)) * block
    o_left, o_right = regroup_call(
        place, out_mine, out_got, ("xyz", "yxz"), ((0, cut), (cut, wide_r))
    )
    d_z.next()
    g_both = Scatter(order, joined(g_left, g_right), "z", both=True)
    order.must(o_left[0], o_right[0])
    a_left.next()
    a_right.next()

    a_left = Scatter(order, a_left.done(ny), "y")
    a_right = Scatter(order, a_right.done(nx), "x")
    o_left = Scatter(order, o_left, "x")
    o_right = Scatter(order, o_right, "y")
    d_z.take()
    g_both.next()
    spill = grad_first[tokens:].reshape(n_rows, HALO, model)[:, HALO - 3 :]
    spill = order.along(spill, -1)
    a_left.next()
    a_right.next()
    o_left.next()
    o_right.next()

    a_both = Scatter(order, joined(a_left, a_right), "z", both=True)
    o_left = Scatter(order, o_left.done(ny), "y")
    o_right = Scatter(order, o_right.done(nx), "x")
    spill = order.wait(spill)
    spill = jnp.pad(spill, ((0, 0), (group - 3, 0), (0, 0))).reshape(tokens, model)
    grad_first = grad_first[:tokens] + spill
    first_pair = order.ring(grad_first[tokens_dev:], "c")
    first_pair = order.wait(first_pair)
    grad_inputs, grad_gain_one = norm_back_call(
        [grad_first[:tokens_dev], first_pair], flat, gains, 0, grad_middle, 0
    )
    order.must(grad_inputs)
    d_x = Scatter(order, d_z.done(ny), "y")
    a_both.next()
    o_left.next()
    o_right.next()
    d_x.next()

    o_both = Scatter(order, joined(o_left, o_right), "z", both=True)
    d_y = Scatter(order, d_x.done(nx), "x")
    g_gains = jnp.concatenate([grad_gain_one, grad_gain_two], axis=0)
    g_gains = jnp.transpose(g_gains.reshape(2, chips, 2, d_rows), (1, 2, 0, 3))
    g_gains = g_gains.reshape(lead + (2, 2 * d_rows))
    g_gains = jnp.moveaxis(behind(place, "yxz", g_gains), 3, 0)
    gains_mine = lax.dynamic_index_in_dim(g_gains, core, 0, False)
    gains_got = order.ring(lax.dynamic_index_in_dim(g_gains, 1 - core, 0, False), "c")
    part_pair = order.ring(part_other, "c")

    def whole_columns(value):
        mine, other = halves(value, place, 0)
        return mine, order.ring(other, "c")

    gains_got, part_pair = order.wait(gains_got, part_pair)
    result = middle + (part + part_pair)
    order.must(result)
    g_gains = gains_mine + gains_got
    g_gains = Scatter(order, [g_gains[i] for i in range(ny)], "y", between=F32)
    a_both.next()
    sum_c = whole_columns(g_both.done(dtype=F32))
    g_gains = Scatter(order, g_gains.done(nx, F32), "x", between=F32)
    o_both.next()
    sum_down = d_y.done(dtype=F32)
    order.must(sum_down)
    g_gains = Scatter(order, g_gains.done(nz, F32), "z", direct=True, between=F32)
    low_c, high_c = place.ordered(sum_c[0], order.wait(sum_c[1]))
    grad_gate = jnp.concatenate([low_c[:, :ffn_half], high_c[:, :ffn_half]], axis=1)
    grad_up = jnp.concatenate([low_c[:, ffn_half:], high_c[:, ffn_half:]], axis=1)
    order.must(grad_gate, grad_up)
    sum_a = whole_columns(a_both.done(dtype=F32))
    o_both.next()
    low_a, high_a = place.ordered(sum_a[0], order.wait(sum_a[1]))
    grad_input_proj = jnp.concatenate([low_a[:, :lru_half], high_a[:, :lru_half]], axis=1)
    grad_branch_proj = jnp.concatenate([low_a[:, lru_half:], high_a[:, lru_half:]], axis=1)
    order.must(grad_input_proj, grad_branch_proj)
    own = o_both.done(dtype=F32)
    g_gains = g_gains.done(dtype=F32).reshape(2, d_rows)
    own_gates = own[:, model : model + 2 * block]
    own_vec = own[:, model + 2 * block : model + 2 * block + 8].T
    return (
        result.reshape(inputs.shape),
        grad_inputs.reshape(inputs.shape),
        g_gains[0],
        grad_input_proj,
        grad_branch_proj,
        own_vec[:4],
        own_vec[4],
        own_gates[:, :block],
        own_gates[:, block:],
        own_vec[5],
        own_vec[6],
        own_vec[7],
        own[:, :model],
        g_gains[1],
        grad_gate,
        grad_up,
        sum_down,
    )


def solution(mesh):
    seq, row = mesh.shape["seq"], mesh.shape["row"]
    ny = 1 << ((seq.bit_length() - 1) // 2)
    grid = Mesh(mesh.devices.reshape(seq // ny, ny, row // 2, 2), AXES)
    tokens, line, flat, taps = P(("x", "c"), ("z", "y"), None), P(AXES, None), P(AXES), P(None, AXES)
    in_specs = (
        tokens,
        tokens,
        P(("x", "c"), ("z", "y")),
        flat,
        line,
        line,
        taps,
        flat,
        line,
        line,
        flat,
        flat,
        flat,
        line,
        flat,
        line,
        line,
        line,
    )
    out_specs = (
        tokens,
        tokens,
        flat,
        line,
        line,
        taps,
        flat,
        line,
        line,
        flat,
        flat,
        flat,
        line,
        flat,
        line,
        line,
        line,
    )
    return jax.shard_map(
        on_device, mesh=grid, in_specs=in_specs, out_specs=out_specs, check_vma=False
    )
```

profile of v0, /device:TPU:0, one launch (start us, length us, event | category | flops | bytes accessed | tf_op | source)
XLA Modules:
  0.0 411.2 jit_solution(2209684672799908908)
XLA Ops:
  11.2 3.0 collective-permute-start
  23.6 2.6 collective-permute-start.5
  30.4 3.0 collective-permute-start.15
  39.0 3.6 collective-permute-start.12
  42.8 2.1 collective-permute-start.11
  44.9 5.2 %collective-permute-done.14 = bf16[1,1,1,72,1536]{4,3,2,1,0:T(8,128)(2,1)S(1)} collective-permute-done((bf16[1,1,1,72,1536]{4,3,2,1,0:T(8,128)(2,1)}, bf16[1,1,1,72,1536]{4,3,2,1,0:T(8,128)(2,1)S(1)}, u32[]{:S(2)}, u32[]{:S(2)}) %collective-permute-start.14) | collective-permute-done | bytes 221216 | tf_op jit(solution)/shard_map/ppermute | solution.py:41
  54.0 6.9 %collective-permute-start.19 = (bf16[1,1,1,64,3072]{4,3,2,1,0:T(8,128)(2,1)}, bf16[1,1,1,64,3072]{4,3,2,1,0:T(8,128)(2,1)}, u32[]{:S(2)}, u32[]{:S(2)}) collective-permute-start(bf16[1,1,1,64,3072]{4,3,2,1,0:T(8,128)(2,1)} %maximum_bitcast_fusion), channel_id=1, source_target_pairs={{0,8},{1,9},{2,10},{3,11},{4,12},{5,13},{6,14},{7,15},{8,16},{9,17... | collective-permute-start | bytes 1179656 | tf_op jit(solution)/shard_map/ppermute | solution.py:41
  60.9 3.1 collective-permute-start.20
  64.0 2.4 collective-permute-done.16
  66.4 4.3 %collective-permute-done.17 = bf16[4,1,1,72,768]{4,3,2,1,0:T(8,128)(2,1)} collective-permute-done((bf16[4,1,1,72,768]{4,3,2,1,0:T(8,128)(2,1)S(1)}, bf16[4,1,1,72,768]{4,3,2,1,0:T(8,128)(2,1)}, u32[]{:S(2)}, u32[]{:S(2)}) %collective-permute-start.17) | collective-permute-done | bytes 442400 | tf_op jit(solution)/shard_map/ppermute | solution.py:41
  76.0 2.5 collective-permute-done.19
  78.5 6.1 %collective-permute-done.20 = bf16[1,1,1,64,3072]{4,3,2,1,0:T(8,128)(2,1)} collective-permute-done((bf16[1,1,1,64,3072]{4,3,2,1,0:T(8,128)(2,1)}, bf16[1,1,1,64,3072]{4,3,2,1,0:T(8,128)(2,1)}, u32[]{:S(2)}, u32[]{:S(2)}) %collective-permute-start.20) | collective-permute-done | bytes 393248 | tf_op jit(solution)/shard_map/ppermute | solution.py:41
  86.1 17.8 %collective-permute-done.18.refs_1_ = bf16[4,2,1,72,768]{4,3,2,1,0:T(8,128)(2,1)} collective-permute-done((bf16[4,2,1,72,768]{4,3,2,1,0:T(8,128)(2,1)S(1)}, bf16[4,2,1,72,768]{4,3,2,1,0:T(8,128)(2,1)}, u32[]{:S(2)}, u32[]{:S(2)}) %collective-permute-start.18) | collective-permute-done | bytes 884768 | tf_op jit(solution)/shard_map/ppermute | solution.py:41
  103.8 3.5 collective-permute-done.21.refs_3_
  117.5 2.3 collective-permute-start.30
  120.1 12.4 %recurrence_forward.1 = (bf16[544,1024]{1,0:T(8,128)(2,1)}, f32[512,768]{1,0:T(8,128)}, bf16[544,768]{1,0:T(8,128)(2,1)}, bf16[512,768]{1,0:T(8,128)(2,1)}, f32[...) custom-call(s32[4]{0:T(128)S(1)} %pad_add_fusion.2.at_ref, ...), custom_call_target="tpu_custom_call" | custom-call | flops 1 | bytes 1 | tf_op jit(solution)/shard_map/recurrence_forward/pallas_call | solution.py:642
  136.2 7.0 %collective-permute-start.26 = (f32[8,768]{1,0:T(8,128)}, f32[8,768]{1,0:T(8,128)S(1)}, u32[]{:S(2)}, u32[]{:S(2)}) collective-permute-start(f32[8,768]{1,0:T(8,128)} %get-tuple-element.271), channel_id=1, source_target_pairs={{0,12},{1,13},{2,14},{3,15},{4,16},{5,17},{6,18},{7,19},{8,20},{9,... | collective-permute-start | bytes 73736 | tf_op jit(solution)/shard_map/ppermute | solution.py:49
  144.9 2.1 broadcast_select_fusion.1
  150.8 5.1 %collective-permute-start.27 = (f32[8,768]{1,0:T(8,128)S(1)}, f32[8,768]{1,0:T(8,128)S(1)}, u32[]{:S(2)}, u32[]{:S(2)}) collective-permute-start(f32[8,768]{1,0:T(8,128)S(1)} %pad_maximum_fusion.25), channel_id=1, source_target_pairs={{0,12},{1,13},{2,14},{3,15},{4,16},{5,17},{6,18},{7,19},{8,20},{9,... | collective-permute-start | bytes 73736 | tf_op jit(solution)/shard_map/ppermute | solution.py:49
  157.5 5.8 %split.1 = (bf16[16,48,1024]{2,1,0:T(8,128)(2,1)}, bf16[16,96,1024]{2,1,0:T(8,128)(2,1)}) custom-call(s32[4]{0:T(128)} %copy-done.34, bf16[32,144,1024]{2,1,0:T(8,128)(2,1)} %bitcast.289), custom_call_target="tpu_custom_call" | custom-call | flops 1 | bytes 1 | tf_op jit(solution)/shard_map/split/pallas_call | solution.py:865
  163.9 6.8 %mix.1 = (f32[512,768]{1,0:T(8,128)}, bf16[512,768]{1,0:T(8,128)(2,1)}, f32[256,1024]{1,0:T(8,128)}, f32[256,1024]{1,0:T(8,128)}) custom-call(f32[512,768]{1,0:T(8,128)} %get-tuple-element.268.local_ref, f32[512,768]{1,0:T(8,128)} %get-tuple-element.269.through_ref, f32[4,768]{1,0:T(4,128)} %fusion.47.enter_ref, f32[512,768]{1,0:T(8,128)} %get-tuple-element.285.bpre_ref, ...), custom_call_target="tpu_custom_call" | custom-call | flops 1 | bytes 1 | tf_op jit(solution)/shard_map/mix/pallas_call | solution.py:712
  170.8 4.1 turn.1
  174.9 8.5 %collective-permute-done.33.refs_1_ = bf16[4,2,1,64,1536]{4,3,2,1,0:T(8,128)(2,1)} collective-permute-done((bf16[4,2,1,64,1536]{4,3,2,1,0:T(8,128)(2,1)}, bf16[4,2,1,64,1536]{4,3,2,1,0:T(8,128)(2,1)}, u32[]{:S(2)}, u32[]{:S(2)}) %collective-permute-start.33) | collective-permute-done | bytes 1572896 | tf_op jit(solution)/shard_map/ppermute | solution.py:41
  183.4 2.3 collective-permute-done.32.refs_3_
  187.5 2.1 collective-permute-done.34.other_ref
  190.4 26.6 %feed_forward.1 = (bf16[512,1536]{1,0:T(8,128)(2,1)}, bf16[512,1536]{1,0:T(8,128)(2,1)}, bf16[512,1536]{1,0:T(8,128)(2,1)}, bf16[512,1536]{1,0:T(8,128)(2,1)}, b...) custom-call(s32[4]{0:T(128)} %copy-done.34, ...), custom_call_target="tpu_custom_call" | custom-call | flops 1 | bytes 1 | tf_op jit(solution)/shard_map/feed_forward/pallas_call | solution.py:819
  219.2 3.2 collective-permute-done.35.refs_1_
  223.6 3.9 norm_back.2
  235.1 7.7 %recurrence_back.1 = (bf16[768,1024]{1,0:T(8,128)(2,1)S(1)}, bf16[512,768]{1,0:T(8,128)(2,1)}, bf16[512,768]{1,0:T(8,128)(2,1)}, bf16[512,768]{1,0:T(8,128)(2,1)...) custom-call(bf16[256,1024]{1,0:T(8,128)(2,1)S(1)} %copy-done.28, ...), custom_call_target="tpu_custom_call" | custom-call | flops 1 | bytes 1 | tf_op jit(solution)/shard_map/recurrence_back/pallas_call | solution.py:997
  244.0 7.9 %collective-permute-done.38 = bf16[2,2,96,1024]{3,2,1,0:T(8,128)(2,1)S(1)} collective-permute-done((bf16[2,2,96,1024]{3,2,1,0:T(8,128)(2,1)S(1)}, bf16[2,2,96,1024]{3,2,1,0:T(8,128)(2,1)S(1)}, u32[]{:S(2)}, u32[]{:S(2)}) %collective-permute-start.38) | collective-permute-done | bytes 786464 | tf_op jit(solution)/shard_map/ppermute | solution.py:41
  253.2 9.8 %collective-permute-start.40 = (f32[8,768]{1,0:T(8,128)S(1)}, f32[8,768]{1,0:T(8,128)S(1)}, u32[]{:S(2)}, u32[]{:S(2)}) collective-permute-start(f32[8,768]{1,0:T(8,128)S(1)} %get-tuple-element.325), channel_id=1, source_target_pairs={{8,0},{9,1},{10,2},{11,3},{12,4},{13,5},{14,6},{15,7},{16,8},{17,9... | collective-permute-start | bytes 73736 | tf_op jit(solution)/shard_map/ppermute | solution.py:49
  264.3 2.7 fusion.3
  266.9 2.8 fusion.1
  274.8 3.2 collective-permute-start.46
  278.0 3.0 collective-permute-done.45
  281.1 15.6 %recurrence_gates.1 = (bf16[512,768]{1,0:T(8,128)(2,1)}, bf16[512,768]{1,0:T(8,128)(2,1)}, f32[768,128]{1,0:T(8,128)S(1)}, f32[768,128]{1,0:T(8,128)S(1)}, f32[8,768]{1,0:T(8,128)S(1)}, /*index=5*/f32[544,1024]{1,0:T(8,128)}) custom-call(f32[512,768]{1,0:T(8,128)S(1)} %get-tuple-element.321.reach_ref, f32[512,768]{1,0:T(8,128)S(1)} %get-tuple-element.322.local_ref, ...), custom_call_target="tpu_custom_call" | custom-call | flops 1 | bytes 1 | tf_op jit(solution)/shard_map/recurrence_gates/pallas_call | solution.py:1157
  298.8 2.1 fusion.24
  303.0 2.8 collective-permute-start.53
  307.2 3.9 collective-permute-start.50
  312.0 9.9 %collective-permute-done.54 = bf16[2,4,64,768]{3,2,1,0:T(8,128)(2,1)S(1)} collective-permute-done((bf16[2,4,64,768]{3,2,1,0:T(8,128)(2,1)S(1)}, bf16[2,4,64,768]{3,2,1,0:T(8,128)(2,1)S(1)}, u32[]{:S(2)}, u32[]{:S(2)}) %collective-permute-start.54) | collective-permute-done | bytes 786464 | tf_op jit(solution)/shard_map/ppermute | solution.py:41
  326.6 2.9 collective-permute-done.52
  330.6 4.2 %collective-permute-done.50 = bf16[64,3072]{1,0:T(8,128)(2,1)S(1)} collective-permute-done((bf16[64,3072]{1,0:T(8,128)(2,1)S(1)}, bf16[64,3072]{1,0:T(8,128)(2,1)S(1)}, u32[]{:S(2)}, u32[]{:S(2)}) %collective-permute-start.50) | collective-permute-done | bytes 393248 | tf_op jit(solution)/shard_map/ppermute | solution.py:41
  336.6 8.6 %collective-permute-done.51 = bf16[64,3072]{1,0:T(8,128)(2,1)S(1)} collective-permute-done((bf16[64,3072]{1,0:T(8,128)(2,1)S(1)}, bf16[64,3072]{1,0:T(8,128)(2,1)S(1)}, u32[]{:S(2)}, u32[]{:S(2)}) %collective-permute-start.51) | collective-permute-done | bytes 393248 | tf_op jit(solution)/shard_map/ppermute | solution.py:41
  356.0 2.6 collective-permute-start.63
  360.7 2.6 fusion.6
  363.3 3.9 collective-permute-start.69
  367.2 3.9 norm_back.3
  374.2 7.2 %collective-permute-done.61 = bf16[2,96,1024]{2,1,0:T(8,128)(2,1)S(1)} collective-permute-done((bf16[2,96,1024]{2,1,0:T(8,128)(2,1)}, bf16[2,96,1024]{2,1,0:T(8,128)(2,1)S(1)}, u32[]{:S(2)}, u32[]{:S(2)}) %collective-permute-start.61) | collective-permute-done | bytes 393248 | tf_op jit(solution)/shard_map/ppermute | solution.py:41
  (439 shorter events, 129.8 us)
Async XLA Ops:
  7.2 150.3 %all-gather.3.cloned.1.call-start = ((), (), s32[]{:S(2)}) async-start(), calls=%async_computation | async-start | bytes 9732096 | tf_op jit(solution)/shard_map/all_gather | solution.py:1297
  15.2 12.4 %collective-permute-start.7 = (s32[2,128]{1,0:T(2,128)}, s32[2,128]{1,0:T(2,128)S(1)}, u32[]{:S(2)}, u32[]{:S(2)}) collective-permute-start(s32[2,128]{1,0:T(2,128)} %param.24), channel_id=1, source_target_pairs={{0,1},{1,0},{2,3},{3,2},{4,5},{5,4},{6,7},{7,6},{8,9},{9,8},{10,11... | collective-permute-start | bytes 3080 | tf_op jit(solution)/shard_map/ppermute | solution.py:41
  15.8 11.8 %collective-permute-start.8 = (bf16[32,3072]{1,0:T(8,128)(2,1)S(1)}, bf16[32,3072]{1,0:T(8,128)(2,1)}, u32[]{:S(2)}, u32[]{:S(2)}) collective-permute-start(bf16[32,3072]{1,0:T(8,128)(2,1)S(1)} %pad_maximum_fusion.12), channel_id=1, source_target_pairs={{0,1},{1,0},{2,3},{3,2},{4,5},{5,4},{6,7},{7,6},{8,9},{9,8},{10,11... | collective-permute-start | bytes 589832 | tf_op jit(solution)/shard_map/ppermute | solution.py:41
  27.6 11.4 %collective-permute-start.10 = (bf16[256,1024]{1,0:T(8,128)(2,1)}, bf16[256,1024]{1,0:T(8,128)(2,1)S(1)}, u32[]{:S(2)}, u32[]{:S(2)}) collective-permute-start(bf16[256,1024]{1,0:T(8,128)(2,1)} %bitcast_convert_fusion.low_mine_ref), channel_id=1, source_target_pairs={{0,1},{1,0},{2,3},{3,2},{4,5},{5,4},{6,7},{7,6},{8,9},{9,8},{10,11... | collective-permute-start | bytes 1572872 | tf_op jit(solution)/shard_map/ppermute | solution.py:41
  27.6 17.3 %collective-permute-start.13 = (bf16[1,1,1,72,1536]{4,3,2,1,0:T(8,128)(2,1)}, bf16[1,1,1,72,1536]{4,3,2,1,0:T(8,128)(2,1)S(1)}, u32[]{:S(2)}, u32[]{:S(2)}) collective-permute-start(bf16[1,1,1,72,1536]{4,3,2,1,0:T(8,128)(2,1)} %maximum_bitcast_fusion.1), channel_id=1, source_target_pairs={{0,8},{1,9},{2,10},{3,11},{4,12},{5,13},{6,14},{7,15},{8,16},{9,17... | collective-permute-start | bytes 663560 | tf_op jit(solution)/shard_map/ppermute | solution.py:41
  28.4 21.6 %collective-permute-start.14 = (bf16[1,1,1,72,1536]{4,3,2,1,0:T(8,128)(2,1)}, bf16[1,1,1,72,1536]{4,3,2,1,0:T(8,128)(2,1)S(1)}, u32[]{:S(2)}, u32[]{:S(2)}) collective-permute-start(bf16[1,1,1,72,1536]{4,3,2,1,0:T(8,128)(2,1)} %maximum_bitcast_fusion.1), channel_id=1, source_target_pairs={{0,16},{1,17},{2,18},{3,19},{4,20},{5,21},{6,22},{7,23},{8,24},{9,... | collective-permute-start | bytes 663560 | tf_op jit(solution)/shard_map/ppermute | solution.py:41
  30.4 19.6 %collective-permute-start.15 = (bf16[1,1,1,72,1536]{4,3,2,1,0:T(8,128)(2,1)}, bf16[1,1,1,72,1536]{4,3,2,1,0:T(8,128)(2,1)S(1)}, u32[]{:S(2)}, u32[]{:S(2)}) collective-permute-start(bf16[1,1,1,72,1536]{4,3,2,1,0:T(8,128)(2,1)} %maximum_bitcast_fusion.1), channel_id=1, source_target_pairs={{0,24},{1,25},{2,26},{3,27},{4,28},{5,29},{6,30},{7,31},{8,0},{9,1... | collective-permute-start | bytes 663560 | tf_op jit(solution)/shard_map/ppermute | solution.py:41
  39.0 12.6 %collective-permute-start.12 = (s32[4,3]{1,0:T(4,128)S(1)}, s32[4,3]{1,0:T(4,128)S(1)}, u32[]{:S(2)}, u32[]{:S(2)}) collective-permute-start(s32[4,3]{1,0:T(4,128)S(1)} %slice.495), channel_id=1, source_target_pairs={{0,4},{1,5},{2,6},{3,7},{4,8},{5,9},{6,10},{7,11},{8,12},{9,13},{1... | collective-permute-start | bytes 152 | tf_op jit(solution)/shard_map/ppermute | solution.py:49
  51.7 14.7 %collective-permute-start.16 = (bf16[4,1,1,72,768]{4,3,2,1,0:T(8,128)(2,1)}, bf16[4,1,1,72,768]{4,3,2,1,0:T(8,128)(2,1)S(1)}, u32[]{:S(2)}, u32[]{:S(2)}) collective-permute-start(bf16[4,1,1,72,768]{4,3,2,1,0:T(8,128)(2,1)} %get-tuple-element.251), channel_id=1, source_target_pairs={{0,4},{1,5},{2,6},{3,7},{4,0},{5,1},{6,2},{7,3},{8,12},{9,13},{10,... | collective-permute-start | bytes 1327112 | tf_op jit(solution)/shard_map/ppermute | solution.py:41
  52.6 18.1 %collective-permute-start.17 = (bf16[4,1,1,72,768]{4,3,2,1,0:T(8,128)(2,1)S(1)}, bf16[4,1,1,72,768]{4,3,2,1,0:T(8,128)(2,1)}, u32[]{:S(2)}, u32[]{:S(2)}) collective-permute-start(bf16[4,1,1,72,768]{4,3,2,1,0:T(8,128)(2,1)S(1)} %get-tuple-element.252), channel_id=1, source_target_pairs={{0,2},{1,3},{2,0},{3,1},{4,6},{5,7},{6,4},{7,5},{8,10},{9,11},{10,... | collective-permute-start | bytes 1327112 | tf_op jit(solution)/shard_map/ppermute | solution.py:41
  54.0 24.5 %collective-permute-start.19 = (bf16[1,1,1,64,3072]{4,3,2,1,0:T(8,128)(2,1)}, bf16[1,1,1,64,3072]{4,3,2,1,0:T(8,128)(2,1)}, u32[]{:S(2)}, u32[]{:S(2)}) collective-permute-start(bf16[1,1,1,64,3072]{4,3,2,1,0:T(8,128)(2,1)} %maximum_bitcast_fusion), channel_id=1, source_target_pairs={{0,8},{1,9},{2,10},{3,11},{4,12},{5,13},{6,14},{7,15},{8,16},{9,17... | collective-permute-start | bytes 1179656 | tf_op jit(solution)/shard_map/ppermute | solution.py:41
  60.9 23.7 %collective-permute-start.20 = (bf16[1,1,1,64,3072]{4,3,2,1,0:T(8,128)(2,1)}, bf16[1,1,1,64,3072]{4,3,2,1,0:T(8,128)(2,1)}, u32[]{:S(2)}, u32[]{:S(2)}) collective-permute-start(bf16[1,1,1,64,3072]{4,3,2,1,0:T(8,128)(2,1)} %maximum_bitcast_fusion), channel_id=1, source_target_pairs={{0,24},{1,25},{2,26},{3,27},{4,28},{5,29},{6,30},{7,31},{8,0},{9,1... | collective-permute-start | bytes 1179656 | tf_op jit(solution)/shard_map/ppermute | solution.py:41
  72.2 31.6 %collective-permute-start.18 = (bf16[4,2,1,72,768]{4,3,2,1,0:T(8,128)(2,1)S(1)}, bf16[4,2,1,72,768]{4,3,2,1,0:T(8,128)(2,1)}, u32[]{:S(2)}, u32[]{:S(2)}) collective-permute-start(bf16[4,2,1,72,768]{4,3,2,1,0:T(8,128)(2,1)S(1)} %pad_maximum_fusion.3.refs_0_), channel_id=1, source_target_pairs={{0,2},{1,3},{2,0},{3,1},{4,6},{5,7},{6,4},{7,5},{8,10},{9,11},{10,... | collective-permute-start | bytes 2654216 | tf_op jit(solution)/shard_map/ppermute | solution.py:41
  73.6 33.7 %collective-permute-start.21 = (bf16[4,1,2,72,768]{4,3,2,1,0:T(8,128)(2,1)}, bf16[4,1,2,72,768]{4,3,2,1,0:T(8,128)(2,1)}, u32[]{:S(2)}, u32[]{:S(2)}) collective-permute-start(bf16[4,1,2,72,768]{4,3,2,1,0:T(8,128)(2,1)} %pad_maximum_fusion.4.refs_2_), channel_id=1, source_target_pairs={{0,4},{1,5},{2,6},{3,7},{4,0},{5,1},{6,2},{7,3},{8,12},{9,13},{10,... | collective-permute-start | bytes 2654216 | tf_op jit(solution)/shard_map/ppermute | solution.py:41
  84.6 26.7 %collective-permute-start.23 = (bf16[1,1,1,64,3072]{4,3,2,1,0:T(8,128)(2,1)}, bf16[1,1,1,64,3072]{4,3,2,1,0:T(8,128)(2,1)S(1)}, u32[]{:S(2)}, u32[]{:S(2)}) collective-permute-start(bf16[1,1,1,64,3072]{4,3,2,1,0:T(8,128)(2,1)} %collective-permute-done.19), channel_id=1, source_target_pairs={{0,8},{1,9},{2,10},{3,11},{4,12},{5,13},{6,14},{7,15},{8,16},{9,17... | collective-permute-start | bytes 1179656 | tf_op jit(solution)/shard_map/ppermute | solution.py:41
  116.2 28.7 %collective-permute-start.29 = (bf16[4,1,1,64,1536]{4,3,2,1,0:T(8,128)(2,1)}, bf16[4,1,1,64,1536]{4,3,2,1,0:T(8,128)(2,1)}, u32[]{:S(2)}, u32[]{:S(2)}) collective-permute-start(bf16[4,1,1,64,1536]{4,3,2,1,0:T(8,128)(2,1)} %get-tuple-element.266), channel_id=1, source_target_pairs={{0,2},{1,3},{2,0},{3,1},{4,6},{5,7},{6,4},{7,5},{8,10},{9,11},{10,... | collective-permute-start | bytes 2359304 | tf_op jit(solution)/shard_map/ppermute | solution.py:41
  117.5 27.5 %collective-permute-start.30 = (bf16[4,1,1,64,1536]{4,3,2,1,0:T(8,128)(2,1)}, bf16[4,1,1,64,1536]{4,3,2,1,0:T(8,128)(2,1)}, u32[]{:S(2)}, u32[]{:S(2)}) collective-permute-start(bf16[4,1,1,64,1536]{4,3,2,1,0:T(8,128)(2,1)} %get-tuple-element.265), channel_id=1, source_target_pairs={{0,4},{1,5},{2,6},{3,7},{4,0},{5,1},{6,2},{7,3},{8,12},{9,13},{10,... | collective-permute-start | bytes 2359304 | tf_op jit(solution)/shard_map/ppermute | solution.py:41
  132.5 10.7 %collective-permute-start.24 = (f32[8,768]{1,0:T(8,128)}, f32[8,768]{1,0:T(8,128)S(1)}, u32[]{:S(2)}, u32[]{:S(2)}) collective-permute-start(f32[8,768]{1,0:T(8,128)} %get-tuple-element.271), channel_id=1, source_target_pairs={{0,4},{1,5},{2,6},{3,7},{4,8},{5,9},{6,10},{7,11},{8,12},{9,13},{1... | collective-permute-start | bytes 73736 | tf_op jit(solution)/shard_map/ppermute | solution.py:49
  148.3 35.1 %collective-permute-start.33 = (bf16[4,2,1,64,1536]{4,3,2,1,0:T(8,128)(2,1)}, bf16[4,2,1,64,1536]{4,3,2,1,0:T(8,128)(2,1)}, u32[]{:S(2)}, u32[]{:S(2)}) collective-permute-start(bf16[4,2,1,64,1536]{4,3,2,1,0:T(8,128)(2,1)} %pad_maximum_fusion.1.refs_0_), channel_id=1, source_target_pairs={{0,2},{1,3},{2,0},{3,1},{4,6},{5,7},{6,4},{7,5},{8,10},{9,11},{10,... | collective-permute-start | bytes 4718600 | tf_op jit(solution)/shard_map/ppermute | solution.py:41
  150.8 35.0 %collective-permute-start.32 = (bf16[4,1,2,64,1536]{4,3,2,1,0:T(8,128)(2,1)}, bf16[4,1,2,64,1536]{4,3,2,1,0:T(8,128)(2,1)}, u32[]{:S(2)}, u32[]{:S(2)}) collective-permute-start(bf16[4,1,2,64,1536]{4,3,2,1,0:T(8,128)(2,1)} %pad_maximum_fusion.2.refs_2_), channel_id=1, source_target_pairs={{0,4},{1,5},{2,6},{3,7},{4,0},{5,1},{6,2},{7,3},{8,12},{9,13},{10,... | collective-permute-start | bytes 4718600 | tf_op jit(solution)/shard_map/ppermute | solution.py:41
  150.8 12.5 %collective-permute-start.27 = (f32[8,768]{1,0:T(8,128)S(1)}, f32[8,768]{1,0:T(8,128)S(1)}, u32[]{:S(2)}, u32[]{:S(2)}) collective-permute-start(f32[8,768]{1,0:T(8,128)S(1)} %pad_maximum_fusion.25), channel_id=1, source_target_pairs={{0,12},{1,13},{2,14},{3,15},{4,16},{5,17},{6,18},{7,19},{8,20},{9,... | collective-permute-start | bytes 73736 | tf_op jit(solution)/shard_map/ppermute | solution.py:49
  170.7 15.1 %collective-permute-start.31 = (f32[256,1024]{1,0:T(8,128)}, f32[256,1024]{1,0:T(8,128)S(1)}, u32[]{:S(2)}, u32[]{:S(2)}) collective-permute-start(f32[256,1024]{1,0:T(8,128)} %get-tuple-element.288), channel_id=1, source_target_pairs={{0,1},{1,0},{2,3},{3,2},{4,5},{5,4},{6,7},{7,6},{8,9},{9,8},{10,11... | collective-permute-start | bytes 3145736 | tf_op jit(solution)/shard_map/ppermute | solution.py:41
  217.1 11.4 %collective-permute-start.37 = (bf16[8,96,1024]{2,1,0:T(8,128)(2,1)}, bf16[8,96,1024]{2,1,0:T(8,128)(2,1)}, u32[]{:S(2)}, u32[]{:S(2)}) collective-permute-start(bf16[8,96,1024]{2,1,0:T(8,128)(2,1)} %get-tuple-element.309), channel_id=1, source_target_pairs={{0,1},{1,0},{2,3},{3,2},{4,5},{5,4},{6,7},{7,6},{8,9},{9,8},{10,11... | collective-permute-start | bytes 4718600 | tf_op jit(solution)/shard_map/ppermute | solution.py:41
  217.6 46.6 %collective-permute-start.43 = (bf16[2,4,64,1536]{3,2,1,0:T(8,128)(2,1)}, bf16[2,4,64,1536]{3,2,1,0:T(8,128)(2,1)}, u32[]{:S(2)}, u32[]{:S(2)}) collective-permute-start(bf16[2,4,64,1536]{3,2,1,0:T(8,128)(2,1)} %bitcast.319), channel_id=1, source_target_pairs={{0,2},{1,3},{2,0},{3,1},{4,6},{5,7},{6,4},{7,5},{8,10},{9,11},{10,... | collective-permute-start | bytes 4718600 | tf_op jit(solution)/shard_map/ppermute | solution.py:41
  218.5 45.8 %collective-permute-start.42 = (bf16[2,4,64,1536]{3,2,1,0:T(8,128)(2,1)}, bf16[2,4,64,1536]{3,2,1,0:T(8,128)(2,1)}, u32[]{:S(2)}, u32[]{:S(2)}) collective-permute-start(bf16[2,4,64,1536]{3,2,1,0:T(8,128)(2,1)} %bitcast.318), channel_id=1, source_target_pairs={{0,4},{1,5},{2,6},{3,7},{4,0},{5,1},{6,2},{7,3},{8,12},{9,13},{10,... | collective-permute-start | bytes 4718600 | tf_op jit(solution)/shard_map/ppermute | solution.py:41
  230.5 21.4 %collective-permute-start.38 = (bf16[2,2,96,1024]{3,2,1,0:T(8,128)(2,1)S(1)}, bf16[2,2,96,1024]{3,2,1,0:T(8,128)(2,1)S(1)}, u32[]{:S(2)}, u32[]{:S(2)}) collective-permute-start(bf16[2,2,96,1024]{3,2,1,0:T(8,128)(2,1)S(1)} %get-tuple-element.316), channel_id=1, source_target_pairs={{0,8},{1,9},{2,10},{3,11},{4,12},{5,13},{6,14},{7,15},{8,16},{9,17... | collective-permute-start | bytes 2359304 | tf_op jit(solution)/shard_map/ppermute | solution.py:41
  251.9 17.9 %collective-permute-start.39 = (f32[8,768]{1,0:T(8,128)S(1)}, f32[8,768]{1,0:T(8,128)S(1)}, u32[]{:S(2)}, u32[]{:S(2)}) collective-permute-start(f32[8,768]{1,0:T(8,128)S(1)} %get-tuple-element.325), channel_id=1, source_target_pairs={{4,0},{5,1},{6,2},{7,3},{8,4},{9,5},{10,6},{11,7},{12,8},{13,9},{1... | collective-permute-start | bytes 73736 | tf_op jit(solution)/shard_map/ppermute | solution.py:49
  253.2 16.6 %collective-permute-start.40 = (f32[8,768]{1,0:T(8,128)S(1)}, f32[8,768]{1,0:T(8,128)S(1)}, u32[]{:S(2)}, u32[]{:S(2)}) collective-permute-start(f32[8,768]{1,0:T(8,128)S(1)} %get-tuple-element.325), channel_id=1, source_target_pairs={{8,0},{9,1},{10,2},{11,3},{12,4},{13,5},{14,6},{15,7},{16,8},{17,9... | collective-permute-start | bytes 73736 | tf_op jit(solution)/shard_map/ppermute | solution.py:49
  273.9 24.9 %collective-permute-start.47 = (bf16[4,64,1536]{2,1,0:T(8,128)(2,1)}, bf16[4,64,1536]{2,1,0:T(8,128)(2,1)}, u32[]{:S(2)}, u32[]{:S(2)}) collective-permute-start(bf16[4,64,1536]{2,1,0:T(8,128)(2,1)} %get-tuple-element.335), channel_id=1, source_target_pairs={{0,2},{1,3},{2,0},{3,1},{4,6},{5,7},{6,4},{7,5},{8,10},{9,11},{10,... | collective-permute-start | bytes 2359304 | tf_op jit(solution)/shard_map/ppermute | solution.py:41
  274.8 24.0 %collective-permute-start.46 = (bf16[4,64,1536]{2,1,0:T(8,128)(2,1)}, bf16[4,64,1536]{2,1,0:T(8,128)(2,1)S(1)}, u32[]{:S(2)}, u32[]{:S(2)}) collective-permute-start(bf16[4,64,1536]{2,1,0:T(8,128)(2,1)} %get-tuple-element.333), channel_id=1, source_target_pairs={{0,4},{1,5},{2,6},{3,7},{4,0},{5,1},{6,2},{7,3},{8,12},{9,13},{10,... | collective-permute-start | bytes 2359304 | tf_op jit(solution)/shard_map/ppermute | solution.py:41
  281.0 20.1 %collective-permute-start.48 = (bf16[2,2,96,1024]{3,2,1,0:T(8,128)(2,1)}, bf16[2,2,96,1024]{3,2,1,0:T(8,128)(2,1)}, u32[]{:S(2)}, u32[]{:S(2)}) collective-permute-start(bf16[2,2,96,1024]{3,2,1,0:T(8,128)(2,1)} %fusion.2), channel_id=1, source_target_pairs={{0,8},{1,9},{2,10},{3,11},{4,12},{5,13},{6,14},{7,15},{8,16},{9,17... | collective-permute-start | bytes 2359304 | tf_op jit(solution)/shard_map/ppermute | solution.py:41
  302.1 19.9 %collective-permute-start.54 = (bf16[2,4,64,768]{3,2,1,0:T(8,128)(2,1)S(1)}, bf16[2,4,64,768]{3,2,1,0:T(8,128)(2,1)S(1)}, u32[]{:S(2)}, u32[]{:S(2)}) collective-permute-start(bf16[2,4,64,768]{3,2,1,0:T(8,128)(2,1)S(1)} %bitcast.322), channel_id=1, source_target_pairs={{0,2},{1,3},{2,0},{3,1},{4,6},{5,7},{6,4},{7,5},{8,10},{9,11},{10,... | collective-permute-start | bytes 2359304 | tf_op jit(solution)/shard_map/ppermute | solution.py:41
  303.0 20.4 %collective-permute-start.53 = (bf16[2,4,64,768]{3,2,1,0:T(8,128)(2,1)S(1)}, bf16[2,4,64,768]{3,2,1,0:T(8,128)(2,1)S(1)}, u32[]{:S(2)}, u32[]{:S(2)}) collective-permute-start(bf16[2,4,64,768]{3,2,1,0:T(8,128)(2,1)S(1)} %bitcast.321), channel_id=1, source_target_pairs={{0,4},{1,5},{2,6},{3,7},{4,0},{5,1},{6,2},{7,3},{8,12},{9,13},{10,... | collective-permute-start | bytes 2359304 | tf_op jit(solution)/shard_map/ppermute | solution.py:41
  307.1 22.3 %collective-permute-start.52 = (bf16[2,2,96,1024]{3,2,1,0:T(8,128)(2,1)S(1)}, bf16[2,2,96,1024]{3,2,1,0:T(8,128)(2,1)S(1)}, u32[]{:S(2)}, u32[]{:S(2)}) collective-permute-start(bf16[2,2,96,1024]{3,2,1,0:T(8,128)(2,1)S(1)} %fusion), channel_id=1, source_target_pairs={{0,8},{1,9},{2,10},{3,11},{4,12},{5,13},{6,14},{7,15},{8,16},{9,17... | collective-permute-start | bytes 2359304 | tf_op jit(solution)/shard_map/ppermute | solution.py:41
  307.2 27.6 %collective-permute-start.50 = (bf16[64,3072]{1,0:T(8,128)(2,1)S(1)}, bf16[64,3072]{1,0:T(8,128)(2,1)S(1)}, u32[]{:S(2)}, u32[]{:S(2)}) collective-permute-start(bf16[64,3072]{1,0:T(8,128)(2,1)S(1)} %pad_maximum_fusion.7), channel_id=1, source_target_pairs={{0,24},{1,25},{2,26},{3,27},{4,28},{5,29},{6,30},{7,31},{8,0},{9,1... | collective-permute-start | bytes 1179656 | tf_op jit(solution)/shard_map/ppermute | solution.py:41
  311.1 34.2 %collective-permute-start.51 = (bf16[64,3072]{1,0:T(8,128)(2,1)S(1)}, bf16[64,3072]{1,0:T(8,128)(2,1)S(1)}, u32[]{:S(2)}, u32[]{:S(2)}) collective-permute-start(bf16[64,3072]{1,0:T(8,128)(2,1)S(1)} %pad_maximum_fusion.8), channel_id=1, source_target_pairs={{0,8},{1,9},{2,10},{3,11},{4,12},{5,13},{6,14},{7,15},{8,16},{9,17... | collective-permute-start | bytes 1179656 | tf_op jit(solution)/shard_map/ppermute | solution.py:41
  323.6 23.8 %collective-permute-start.56 = (bf16[2,4,48,768]{3,2,1,0:T(8,128)(2,1)S(1)}, bf16[2,4,48,768]{3,2,1,0:T(8,128)(2,1)S(1)}, u32[]{:S(2)}, u32[]{:S(2)}) collective-permute-start(bf16[2,4,48,768]{3,2,1,0:T(8,128)(2,1)S(1)} %get-tuple-element.374), channel_id=1, source_target_pairs={{0,4},{1,5},{2,6},{3,7},{4,0},{5,1},{6,2},{7,3},{8,12},{9,13},{10,... | collective-permute-start | bytes 1769480 | tf_op jit(solution)/shard_map/ppermute | solution.py:41
  325.4 22.0 %collective-permute-start.57 = (bf16[2,4,48,640]{3,2,1,0:T(8,128)(2,1)S(1)}, bf16[2,4,48,640]{3,2,1,0:T(8,128)(2,1)S(1)}, u32[]{:S(2)}, u32[]{:S(2)}) collective-permute-start(bf16[2,4,48,640]{3,2,1,0:T(8,128)(2,1)S(1)} %get-tuple-element.373), channel_id=1, source_target_pairs={{0,2},{1,3},{2,0},{3,1},{4,6},{5,7},{6,4},{7,5},{8,10},{9,11},{10,... | collective-permute-start | bytes 1474568 | tf_op jit(solution)/shard_map/ppermute | solution.py:41
  329.4 18.0 %collective-permute-start.58 = (bf16[4,64,768]{2,1,0:T(8,128)(2,1)S(1)}, bf16[4,64,768]{2,1,0:T(8,128)(2,1)S(1)}, u32[]{:S(2)}, u32[]{:S(2)}) collective-permute-start(bf16[4,64,768]{2,1,0:T(8,128)(2,1)S(1)} %get-tuple-element.372), channel_id=1, source_target_pairs={{0,2},{1,3},{2,0},{3,1},{4,6},{5,7},{6,4},{7,5},{8,10},{9,11},{10,... | collective-permute-start | bytes 1179656 | tf_op jit(solution)/shard_map/ppermute | solution.py:41
  334.8 12.6 %collective-permute-start.59 = (bf16[4,64,768]{2,1,0:T(8,128)(2,1)S(1)}, bf16[4,64,768]{2,1,0:T(8,128)(2,1)S(1)}, u32[]{:S(2)}, u32[]{:S(2)}) collective-permute-start(bf16[4,64,768]{2,1,0:T(8,128)(2,1)S(1)} %get-tuple-element.370), channel_id=1, source_target_pairs={{0,4},{1,5},{2,6},{3,7},{4,0},{5,1},{6,2},{7,3},{8,12},{9,13},{10,... | collective-permute-start | bytes 1179656 | tf_op jit(solution)/shard_map/ppermute | solution.py:41
  354.9 18.2 %collective-permute-start.62 = (bf16[4,48,768]{2,1,0:T(8,128)(2,1)}, bf16[4,48,768]{2,1,0:T(8,128)(2,1)}, u32[]{:S(2)}, u32[]{:S(2)}) collective-permute-start(bf16[4,48,768]{2,1,0:T(8,128)(2,1)} %get-tuple-element.389), channel_id=1, source_target_pairs={{0,2},{1,3},{2,0},{3,1},{4,6},{5,7},{6,4},{7,5},{8,10},{9,11},{10,... | collective-permute-start | bytes 884744 | tf_op jit(solution)/shard_map/ppermute | solution.py:41
  356.0 17.0 %collective-permute-start.63 = (bf16[4,48,640]{2,1,0:T(8,128)(2,1)}, bf16[4,48,640]{2,1,0:T(8,128)(2,1)}, u32[]{:S(2)}, u32[]{:S(2)}) collective-permute-start(bf16[4,48,640]{2,1,0:T(8,128)(2,1)} %get-tuple-element.387), channel_id=1, source_target_pairs={{0,4},{1,5},{2,6},{3,7},{4,0},{5,1},{6,2},{7,3},{8,12},{9,13},{10,... | collective-permute-start | bytes 737288 | tf_op jit(solution)/shard_map/ppermute | solution.py:41
  358.7 12.4 %collective-permute-start.64 = (bf16[64,1536]{1,0:T(8,128)(2,1)}, bf16[64,1536]{1,0:T(8,128)(2,1)S(1)}, u32[]{:S(2)}, u32[]{:S(2)}) collective-permute-start(bf16[64,1536]{1,0:T(8,128)(2,1)} %pad_maximum_fusion.14), channel_id=1, source_target_pairs={{0,24},{1,25},{2,26},{3,27},{4,28},{5,29},{6,30},{7,31},{8,0},{9,1... | collective-permute-start | bytes 589832 | tf_op jit(solution)/shard_map/ppermute | solution.py:41
  360.6 11.3 %collective-permute-start.65 = (bf16[64,1536]{1,0:T(8,128)(2,1)}, bf16[64,1536]{1,0:T(8,128)(2,1)S(1)}, u32[]{:S(2)}, u32[]{:S(2)}) collective-permute-start(bf16[64,1536]{1,0:T(8,128)(2,1)} %pad_maximum_fusion.15), channel_id=1, source_target_pairs={{0,8},{1,9},{2,10},{3,11},{4,12},{5,13},{6,14},{7,15},{8,16},{9,17... | collective-permute-start | bytes 589832 | tf_op jit(solution)/shard_map/ppermute | solution.py:41
  363.3 25.2 %collective-permute-start.69 = (bf16[64,3072]{1,0:T(8,128)(2,1)}, bf16[64,3072]{1,0:T(8,128)(2,1)}, u32[]{:S(2)}, u32[]{:S(2)}) collective-permute-start(bf16[64,3072]{1,0:T(8,128)(2,1)} %add_convert_fusion), channel_id=1, source_target_pairs={{0,24},{1,25},{2,26},{3,27},{4,28},{5,29},{6,30},{7,31},{8,0},{9,1... | collective-permute-start | bytes 1179656 | tf_op jit(solution)/shard_map/ppermute | solution.py:41
  371.0 10.3 %collective-permute-start.61 = (bf16[2,96,1024]{2,1,0:T(8,128)(2,1)}, bf16[2,96,1024]{2,1,0:T(8,128)(2,1)S(1)}, u32[]{:S(2)}, u32[]{:S(2)}) collective-permute-start(bf16[2,96,1024]{2,1,0:T(8,128)(2,1)} %get-tuple-element.396), channel_id=1, source_target_pairs={{0,4},{1,5},{2,6},{3,7},{4,0},{5,1},{6,2},{7,3},{8,12},{9,13},{10,... | collective-permute-start | bytes 1179656 | tf_op jit(solution)/shard_map/ppermute | solution.py:41
  372.9 14.5 %collective-permute-start.70 = (bf16[64,1536]{1,0:T(8,128)(2,1)}, bf16[64,1536]{1,0:T(8,128)(2,1)S(1)}, u32[]{:S(2)}, u32[]{:S(2)}) collective-permute-start(bf16[64,1536]{1,0:T(8,128)(2,1)} %add_convert_fusion.5), channel_id=1, source_target_pairs={{0,24},{1,25},{2,26},{3,27},{4,28},{5,29},{6,30},{7,31},{8,0},{9,1... | collective-permute-start | bytes 589832 | tf_op jit(solution)/shard_map/ppermute | solution.py:41
  383.2 11.4 %collective-permute-start.72 = (bf16[96,1024]{1,0:T(8,128)(2,1)S(1)}, bf16[96,1024]{1,0:T(8,128)(2,1)S(1)}, u32[]{:S(2)}, u32[]{:S(2)}) collective-permute-start(bf16[96,1024]{1,0:T(8,128)(2,1)S(1)} %fusion.22), channel_id=1, source_target_pairs={{0,2},{1,3},{2,0},{3,1},{4,6},{5,7},{6,4},{7,5},{8,10},{9,11},{10,... | collective-permute-start | bytes 589832 | tf_op jit(solution)/shard_map/ppermute | solution.py:41
  (113 other events, 988.9 us)
Sparse Core Ops, SparseCore 0:
  11.5 113.5 all-gather.2
where the time goes:
time: 418 us; the launch traced here: 411 us
  starting transfers between devices  118 us (28%)
  waiting for transfers between devices  110 us (26%)
  Pallas kernels  94.9 us (23%)
  other arithmetic  51.9 us (12%)
  local copies, waits for them, and re-layouts  20 us (5%)
  between operations  16 us (4%)
    ppermute x68, waiting for transfers between devices, ring(): return lax.ppermute(value, AXES, pairs)  105 us
    ppermute x68, starting transfers between devices, ring(): return lax.ppermute(value, AXES, pairs)  78.8 us
    ppermute x13, starting transfers between devices, along(): return lax.ppermute(value, AXES, pairs)  39.5 us
    pallas_call x1, Pallas kernels, ffn_call(): pl.pallas_call(functools.partial(ffn_kernel, place.sizes, chip_d, len(w_g...  26.6 us
    convert_element_type x14, other arithmetic, total(): return functools.reduce(jnp.add, values).astype(dtype)  17.1 us
    pallas_call x1, Pallas kernels, gates_call(): pl.pallas_call(functools.partial(gates_kernel, n_rows, group, block), gri...  15.6 us
    pallas_call x1, Pallas kernels, forward_call(): pl.pallas_call(functools.partial(forward_kernel, n_rows, group, block, le...  12.4 us
  transfers between devices with their start and end apart: 82, of which 26 were waited for; matrix products, arithmetic and copies ran while one was open for 15% of the time, Pallas kernels for 16%

commit v1 on v0

--- a/solution.py
+++ b/solution.py
@@ -1052,27 +1052,22 @@
     gr_ref,
     gi_ref,
     left_ref,
-    win_ref,
-    wbr_ref,
-    gbl_ref,
     gin_send_ref,
     gin_ref,
     ggr_ref,
     ggi_ref,
     gvec_ref,
-    gfirst_ref,
+    gm_ref,
     rlow_ref,
     ilow_ref,
     gconv_ref,
     ext_ref,
     spread_ref,
-    gm_ref,
 ):
-    step = pl.program_id(0)
     tokens = n_rows * group
 
     gvec_ref[...] = jnp.zeros_like(gvec_ref)
-    for h in range(win_ref.shape[1] // block):
+    for h in range(conv_ref.shape[1] // block):
         cols = slice(h * block, (h + 1) * block)
         for r in range(n_rows):
             span = slice(r * group, (r + 1) * group)
@@ -1132,6 +1127,12 @@
     gin = dot(left_ref[...], gm).astype(BF)
     gin_send_ref[...] = gin[:sent]
     gin_ref[...] = gin[sent:]
+
+
+def first_kernel(gm_ref, gbl_ref, win_ref, wbr_ref, gfirst_ref):
+    step = pl.program_id(0)
+    tokens = gbl_ref.shape[0]
+    gm = gm_ref[...]
     part = dot_nt(gm, win_ref[...])
     part_branch = dot_nt(gbl_ref[...], wbr_ref[...])
 
@@ -1147,7 +1148,7 @@
 
 
 def gates_call(
-    place, reach, local, leave, state, enter, rpre, ipre, conv, mixer, vec, masks, gate_r, gate_i, left, w_in, w_branch, gbl, n_rows, group
+    place, reach, local, leave, state, enter, rpre, ipre, conv, mixer, vec, masks, gate_r, gate_i, left, n_rows, group
 ):
     model, length = left.shape
     sent = model // place.size["x"]
@@ -1172,9 +1173,6 @@
             lines(tile, block),
             lines(tile, block),
             full((model, length)),
-            columns(model),
-            columns(model),
-            columns(tokens),
         ],
         out_specs=[
             columns(sent),
@@ -1182,7 +1180,7 @@
             lines(tile, block),
             lines(tile, block),
             columns(8),
-            full((length, model)),
+            columns(length),
         ],
         out_shape=[
             in_hbm((sent, width), BF),
@@ -1190,7 +1188,7 @@
             shape_of((width, block), F32),
             shape_of((width, block), F32),
             shape_of((8, width), F32),
-            shape_of((length, model), F32),
+            in_hbm((length, width), BF),
         ],
         scratch_shapes=[
             pltpu.VMEM((tokens, tile), BF),
@@ -1198,12 +1196,26 @@
             pltpu.VMEM((tokens, tile), F32),
             pltpu.VMEM((HALO + group, block), F32),
             pltpu.VMEM((HALO + group, block), F32),
-            pltpu.VMEM((length, tile), BF),
         ],
         compiler_params=params(40),
         cost_estimate=LIGHT,
         name="recurrence_gates",
-    )(reach, local, leave, state, enter, rpre, ipre, conv, mixer, vec, masks, gate_r, gate_i, left, w_in, w_branch, gbl)
+    )(reach, local, leave, state, enter, rpre, ipre, conv, mixer, vec, masks, gate_r, gate_i, left)
+
+
+def first_call(gm, gbl, w_in, w_branch):
+    length, width = gm.shape
+    model = w_in.shape[0]
+    return pl.pallas_call(
+        first_kernel,
+        grid=(width // TILE,),
+        in_specs=[columns(length), columns(gbl.shape[0]), columns(model), columns(model)],
+        out_specs=full((length, model)),
+        out_shape=shape_of((length, model), F32),
+        compiler_params=params(24),
+        cost_estimate=LIGHT,
+        name="first_gradient",
+    )(gm, gbl, w_in, w_branch)
 
 
 def normed(values, gain):
@@ -1422,16 +1434,16 @@
     g_right = Scatter(order, g_right.done(nx), "x")
     leave = leave.done() if more else leave.total[4:]
     d_z.next()
-    in_send, in_rest, g_gate_r, g_gate_i, g_vec, grad_first = gates_call(
-        place, reach, local_back, leave, state, enter, rpre, ipre, conv, mixer, vec, masks, gate_r, gate_i, first_l, w_in, w_branch, gbl, n_rows, group
+    in_send, in_rest, g_gate_r, g_gate_i, g_vec, gm = gates_call(
+        place, reach, local_back, leave, state, enter, rpre, ipre, conv, mixer, vec, masks, gate_r, gate_i, first_l, n_rows, group
     )
     order.must(in_send)
     g_left.next()
     g_right.next()
-    d_z.take()
 
     a_left = Scatter(order, blocks_of(in_send, in_rest, "x", "y"), "x")
     a_right = Scatter(order, blocks_of(b_send, b_rest, "y", "x"), "y")
+    d_z.take()
     out_mine, out_other = pack_call(place, g_out, g_gate_r, g_gate_i, g_vec, vec, r_rows)
     out_got = order.ring(out_other, "c")
     out_got = order.wait(out_got)
@@ -1441,7 +1453,9 @@
         place, out_mine, out_got, ("xyz", "yxz"), ((0, cut), (cut, wide_r))
     )
     d_z.next()
-    g_both = Scatter(order, joined(g_left, g_right), "z", both=True)
+    grad_first = first_call(order.tie(gm), gbl, w_in, w_branch)
+    order.must(grad_first)
+    g_both = Scatter(order, joined(g_left, g_right), "z")
     order.must(o_left[0], o_right[0])
     a_left.next()
     a_right.next()
@@ -1471,6 +1485,7 @@
         [grad_first[:tokens_dev], first_pair], flat, gains, 0, grad_middle, 0
     )
     order.must(grad_inputs)
+    g_both.next()
     d_x = Scatter(order, d_z.done(ny), "y")
     a_both.next()
     o_left.next()

time: 418 us -> 412 us (0.986)
  starting transfers between devices: 118 us -> 110 us
    ppermute x68, starting transfers between devices: 78.8 us -> 71.1 us  [ring(): return lax.ppermute(value, AXES, pairs)]
    ppermute x13, waiting for transfers between devices: 4.73 us -> 9.71 us  [along(): return lax.ppermute(value, AXES, pairs)]
    pallas_call x1, Pallas kernels: 15.6 us -> 11.4 us  [gates_call(): pl.pallas_call(functools.partial(gates_kernel, n_rows, group, block), gri...]
  transfers between devices with their start and end apart: 82 -> 82, of which waited for: 26 -> 30; matrix products, arithmetic and copies ran while one was open for 15% -> 15% of each run, Pallas kernels for 16% -> 16%
where the time goes in v1:
time: 412 us; the launch traced here: 406 us
  waiting for transfers between devices  114 us (28%)
  starting transfers between devices  110 us (27%)
  Pallas kernels  94.7 us (23%)
  other arithmetic  53.1 us (13%)
  local copies, waits for them, and re-layouts  17.9 us (4%)
  between operations  16.1 us (4%)
    ppermute x68, waiting for transfers between devices, ring(): return lax.ppermute(value, AXES, pairs)  104 us
    ppermute x68, starting transfers between devices, ring(): return lax.ppermute(value, AXES, pairs)  71.1 us
    ppermute x13, starting transfers between devices, along(): return lax.ppermute(value, AXES, pairs)  39.2 us
    pallas_call x1, Pallas kernels, ffn_call(): pl.pallas_call(functools.partial(ffn_kernel, place.sizes, chip_d, len(w_g...  26.6 us
    convert_element_type x14, other arithmetic, total(): return functools.reduce(jnp.add, values).astype(dtype)  16.5 us
    pallas_call x1, Pallas kernels, forward_call(): pl.pallas_call(functools.partial(forward_kernel, n_rows, group, block, le...  12.4 us
    pallas_call x1, Pallas kernels, gates_call(): pl.pallas_call(functools.partial(gates_kernel, n_rows, group, block), gri...  11.4 us
    ppermute x13, waiting for transfers between devices, along(): return lax.ppermute(value, AXES, pairs)  9.71 us
  transfers between devices with their start and end apart: 82, of which 30 were waited for; matrix products, arithmetic and copies ran while one was open for 15% of the time, Pallas kernels for 16%

profile of v1, /device:TPU:0, one launch (start us, length us, event | category | flops | bytes accessed | tf_op | source)
XLA Modules:
  0.0 406.0 jit_solution(13615008745562921112)
XLA Ops:
  11.2 3.0 collective-permute-start
  23.6 2.6 collective-permute-start.5
  30.4 3.1 collective-permute-start.15
  39.1 3.6 collective-permute-start.12
  44.7 5.4 %collective-permute-done.14 = bf16[1,1,1,72,1536]{4,3,2,1,0:T(8,128)(2,1)S(1)} collective-permute-done((bf16[1,1,1,72,1536]{4,3,2,1,0:T(8,128)(2,1)}, bf16[1,1,1,72,1536]{4,3,2,1,0:T(8,128)(2,1)S(1)}, u32[]{:S(2)}, u32[]{:S(2)}) %collective-permute-start.14) | collective-permute-done | bytes 221216 | tf_op jit(solution)/shard_map/ppermute | solution.py:41
  54.0 6.9 %collective-permute-start.19 = (bf16[1,1,1,64,3072]{4,3,2,1,0:T(8,128)(2,1)}, bf16[1,1,1,64,3072]{4,3,2,1,0:T(8,128)(2,1)}, u32[]{:S(2)}, u32[]{:S(2)}) collective-permute-start(bf16[1,1,1,64,3072]{4,3,2,1,0:T(8,128)(2,1)} %maximum_bitcast_fusion), channel_id=1, source_target_pairs={{0,8},{1,9},{2,10},{3,11},{4,12},{5,13},{6,14},{7,15},{8,16},{9,17... | collective-permute-start | bytes 1179656 | tf_op jit(solution)/shard_map/ppermute | solution.py:41
  60.9 3.1 collective-permute-start.20
  64.0 2.4 collective-permute-done.16
  66.4 4.3 %collective-permute-done.17 = bf16[4,1,1,72,768]{4,3,2,1,0:T(8,128)(2,1)} collective-permute-done((bf16[4,1,1,72,768]{4,3,2,1,0:T(8,128)(2,1)S(1)}, bf16[4,1,1,72,768]{4,3,2,1,0:T(8,128)(2,1)}, u32[]{:S(2)}, u32[]{:S(2)}) %collective-permute-start.17) | collective-permute-done | bytes 442400 | tf_op jit(solution)/shard_map/ppermute | solution.py:41
  76.0 2.5 collective-permute-done.19
  78.5 6.1 %collective-permute-done.20 = bf16[1,1,1,64,3072]{4,3,2,1,0:T(8,128)(2,1)} collective-permute-done((bf16[1,1,1,64,3072]{4,3,2,1,0:T(8,128)(2,1)}, bf16[1,1,1,64,3072]{4,3,2,1,0:T(8,128)(2,1)}, u32[]{:S(2)}, u32[]{:S(2)}) %collective-permute-start.20) | collective-permute-done | bytes 393248 | tf_op jit(solution)/shard_map/ppermute | solution.py:41
  86.1 17.8 %collective-permute-done.18.refs_1_ = bf16[4,2,1,72,768]{4,3,2,1,0:T(8,128)(2,1)} collective-permute-done((bf16[4,2,1,72,768]{4,3,2,1,0:T(8,128)(2,1)S(1)}, bf16[4,2,1,72,768]{4,3,2,1,0:T(8,128)(2,1)}, u32[]{:S(2)}, u32[]{:S(2)}) %collective-permute-start.18) | collective-permute-done | bytes 884768 | tf_op jit(solution)/shard_map/ppermute | solution.py:41
  103.8 3.6 collective-permute-done.21.refs_3_
  117.5 2.3 collective-permute-start.30
  120.1 12.4 %recurrence_forward.1 = (bf16[544,1024]{1,0:T(8,128)(2,1)}, f32[512,768]{1,0:T(8,128)}, bf16[544,768]{1,0:T(8,128)(2,1)}, bf16[512,768]{1,0:T(8,128)(2,1)}, f32[...) custom-call(s32[4]{0:T(128)S(1)} %pad_add_fusion.2.at_ref, ...), custom_call_target="tpu_custom_call" | custom-call | flops 1 | bytes 1 | tf_op jit(solution)/shard_map/recurrence_forward/pallas_call | solution.py:642
  136.2 6.9 %collective-permute-start.26 = (f32[8,768]{1,0:T(8,128)}, f32[8,768]{1,0:T(8,128)S(1)}, u32[]{:S(2)}, u32[]{:S(2)}) collective-permute-start(f32[8,768]{1,0:T(8,128)} %get-tuple-element.272), channel_id=1, source_target_pairs={{0,12},{1,13},{2,14},{3,15},{4,16},{5,17},{6,18},{7,19},{8,20},{9,... | collective-permute-start | bytes 73736 | tf_op jit(solution)/shard_map/ppermute | solution.py:49
  145.0 2.1 broadcast_select_fusion.1
  150.8 5.1 %collective-permute-start.27 = (f32[8,768]{1,0:T(8,128)S(1)}, f32[8,768]{1,0:T(8,128)S(1)}, u32[]{:S(2)}, u32[]{:S(2)}) collective-permute-start(f32[8,768]{1,0:T(8,128)S(1)} %pad_maximum_fusion.24), channel_id=1, source_target_pairs={{0,12},{1,13},{2,14},{3,15},{4,16},{5,17},{6,18},{7,19},{8,20},{9,... | collective-permute-start | bytes 73736 | tf_op jit(solution)/shard_map/ppermute | solution.py:49
  157.5 5.7 %split.1 = (bf16[16,48,1024]{2,1,0:T(8,128)(2,1)}, bf16[16,96,1024]{2,1,0:T(8,128)(2,1)}) custom-call(s32[4]{0:T(128)} %copy-done.37, bf16[32,144,1024]{2,1,0:T(8,128)(2,1)} %bitcast.289), custom_call_target="tpu_custom_call" | custom-call | flops 1 | bytes 1 | tf_op jit(solution)/shard_map/split/pallas_call | solution.py:865
  163.8 6.8 %mix.1 = (f32[512,768]{1,0:T(8,128)}, bf16[512,768]{1,0:T(8,128)(2,1)}, f32[256,1024]{1,0:T(8,128)}, f32[256,1024]{1,0:T(8,128)}) custom-call(f32[512,768]{1,0:T(8,128)} %get-tuple-element.269.local_ref, f32[512,768]{1,0:T(8,128)} %get-tuple-element.270.through_ref, f32[4,768]{1,0:T(4,128)} %fusion.47.enter_ref, f32[512,768]{1,0:T(8,128)} %get-tuple-element.286.bpre_ref, ...), custom_call_target="tpu_custom_call" | custom-call | flops 1 | bytes 1 | tf_op jit(solution)/shard_map/mix/pallas_call | solution.py:712
  170.7 4.1 %turn.1 = (bf16[1024,544]{1,0:T(8,128)(2,1)S(1)}, bf16[1024,544]{1,0:T(8,128)(2,1)S(1)}) custom-call(s32[4]{0:T(128)S(1)} %copy-done.38, bf16[544,1024]{1,0:T(8,128)(2,1)S(1)} %copy-done.20), custom_call_target="tpu_custom_call" | custom-call | flops 1 | bytes 1 | tf_op jit(solution)/shard_map/turn/pallas_call | solution.py:417
  174.8 8.6 %collective-permute-done.33.refs_1_ = bf16[4,2,1,64,1536]{4,3,2,1,0:T(8,128)(2,1)} collective-permute-done((bf16[4,2,1,64,1536]{4,3,2,1,0:T(8,128)(2,1)}, bf16[4,2,1,64,1536]{4,3,2,1,0:T(8,128)(2,1)}, u32[]{:S(2)}, u32[]{:S(2)}) %collective-permute-start.33) | collective-permute-done | bytes 1572896 | tf_op jit(solution)/shard_map/ppermute | solution.py:41
  183.4 2.4 collective-permute-done.32.refs_3_
  187.5 2.1 collective-permute-done.34.other_ref
  190.5 26.6 %feed_forward.1 = (bf16[512,1536]{1,0:T(8,128)(2,1)}, bf16[512,1536]{1,0:T(8,128)(2,1)}, bf16[512,1536]{1,0:T(8,128)(2,1)}, bf16[512,1536]{1,0:T(8,128)(2,1)}, b...) custom-call(s32[4]{0:T(128)} %copy-done.37, ...), custom_call_target="tpu_custom_call" | custom-call | flops 1 | bytes 1 | tf_op jit(solution)/shard_map/feed_forward/pallas_call | solution.py:819
  219.2 3.2 collective-permute-done.35.refs_1_
  223.7 3.9 norm_back.2
  235.2 7.6 %recurrence_back.1 = (bf16[768,1024]{1,0:T(8,128)(2,1)S(1)}, bf16[512,768]{1,0:T(8,128)(2,1)}, bf16[512,768]{1,0:T(8,128)(2,1)}, bf16[512,768]{1,0:T(8,128)(2,1)...) custom-call(bf16[256,1024]{1,0:T(8,128)(2,1)S(1)} %copy-done.31, ...), custom_call_target="tpu_custom_call" | custom-call | flops 1 | bytes 1 | tf_op jit(solution)/shard_map/recurrence_back/pallas_call | solution.py:997
  242.8 9.1 %collective-permute-done.38 = bf16[2,2,96,1024]{3,2,1,0:T(8,128)(2,1)S(1)} collective-permute-done((bf16[2,2,96,1024]{3,2,1,0:T(8,128)(2,1)S(1)}, bf16[2,2,96,1024]{3,2,1,0:T(8,128)(2,1)S(1)}, u32[]{:S(2)}, u32[]{:S(2)}) %collective-permute-start.38) | collective-permute-done | bytes 786464 | tf_op jit(solution)/shard_map/ppermute | solution.py:41
  254.6 9.9 %collective-permute-start.41 = (f32[8,768]{1,0:T(8,128)S(1)}, f32[8,768]{1,0:T(8,128)S(1)}, u32[]{:S(2)}, u32[]{:S(2)}) collective-permute-start(f32[8,768]{1,0:T(8,128)S(1)} %get-tuple-element.326), channel_id=1, source_target_pairs={{12,0},{13,1},{14,2},{15,3},{16,4},{17,5},{18,6},{19,7},{20,8},{21... | collective-permute-start | bytes 73736 | tf_op jit(solution)/shard_map/ppermute | solution.py:49
  268.2 3.4 collective-permute-done.41
  279.3 3.4 collective-permute-done.45
  282.8 11.4 %recurrence_gates.1 = (bf16[512,768]{1,0:T(8,128)(2,1)}, bf16[512,768]{1,0:T(8,128)(2,1)}, f32[768,128]{1,0:T(8,128)S(1)}, f32[768,128]{1,0:T(8,128)S(1)}, f32[8...) custom-call(f32[512,768]{1,0:T(8,128)S(1)} %get-tuple-element.322.reach_ref, f32[512,768]{1,0:T(8,128)S(1)} %get-tuple-element.323.local_ref, ...), custom_call_target="tpu_custom_call" | custom-call | flops 1 | bytes 1 | tf_op jit(solution)/shard_map/recurrence_gates/pallas_call | solution.py:1158
  297.2 3.5 collective-permute-done.46
  300.7 2.1 fusion.24
  302.9 2.2 fusion.23
  308.2 4.0 first_gradient.1
  315.8 13.0 %collective-permute-done.51 = bf16[2,2,96,1024]{3,2,1,0:T(8,128)(2,1)S(1)} collective-permute-done((bf16[2,2,96,1024]{3,2,1,0:T(8,128)(2,1)S(1)}, bf16[2,2,96,1024]{3,2,1,0:T(8,128)(2,1)S(1)}, u32[]{:S(2)}, u32[]{:S(2)}) %collective-permute-start.51) | collective-permute-done | bytes 786464 | tf_op jit(solution)/shard_map/ppermute | solution.py:41
  329.2 7.7 %collective-permute-done.50 = bf16[64,3072]{1,0:T(8,128)(2,1)S(1)} collective-permute-done((bf16[64,3072]{1,0:T(8,128)(2,1)S(1)}, bf16[64,3072]{1,0:T(8,128)(2,1)S(1)}, u32[]{:S(2)}, u32[]{:S(2)}) %collective-permute-start.50) | collective-permute-done | bytes 393248 | tf_op jit(solution)/shard_map/ppermute | solution.py:41
  345.7 2.3 collective-permute-start.60
  349.1 3.7 collective-permute-start.64
  352.8 2.5 fusion.6
  355.7 3.9 norm_back.3
  359.8 2.5 collective-permute-start.61
  364.4 3.4 collective-permute-done.65
  373.8 3.0 collective-permute-start.73
  378.1 3.1 collective-permute-done.70
  381.2 2.2 collective-permute-start.68
  (450 shorter events, 129.6 us)
Async XLA Ops:
  7.2 150.3 %all-gather.3.cloned.1.call-start = ((), (), s32[]{:S(2)}) async-start(), calls=%async_computation | async-start | bytes 9732096 | tf_op jit(solution)/shard_map/all_gather | solution.py:1309
  15.2 12.4 %collective-permute-start.7 = (s32[2,128]{1,0:T(2,128)}, s32[2,128]{1,0:T(2,128)S(1)}, u32[]{:S(2)}, u32[]{:S(2)}) collective-permute-start(s32[2,128]{1,0:T(2,128)} %param.24), channel_id=1, source_target_pairs={{0,1},{1,0},{2,3},{3,2},{4,5},{5,4},{6,7},{7,6},{8,9},{9,8},{10,11... | collective-permute-start | bytes 3080 | tf_op jit(solution)/shard_map/ppermute | solution.py:41
  15.8 11.8 %collective-permute-start.8 = (bf16[32,3072]{1,0:T(8,128)(2,1)S(1)}, bf16[32,3072]{1,0:T(8,128)(2,1)}, u32[]{:S(2)}, u32[]{:S(2)}) collective-permute-start(bf16[32,3072]{1,0:T(8,128)(2,1)S(1)} %pad_maximum_fusion.11), channel_id=1, source_target_pairs={{0,1},{1,0},{2,3},{3,2},{4,5},{5,4},{6,7},{7,6},{8,9},{9,8},{10,11... | collective-permute-start | bytes 589832 | tf_op jit(solution)/shard_map/ppermute | solution.py:41
  27.6 11.5 %collective-permute-start.10 = (bf16[256,1024]{1,0:T(8,128)(2,1)}, bf16[256,1024]{1,0:T(8,128)(2,1)S(1)}, u32[]{:S(2)}, u32[]{:S(2)}) collective-permute-start(bf16[256,1024]{1,0:T(8,128)(2,1)} %bitcast_convert_fusion.low_mine_ref), channel_id=1, source_target_pairs={{0,1},{1,0},{2,3},{3,2},{4,5},{5,4},{6,7},{7,6},{8,9},{9,8},{10,11... | collective-permute-start | bytes 1572872 | tf_op jit(solution)/shard_map/ppermute | solution.py:41
  27.6 17.1 %collective-permute-start.13 = (bf16[1,1,1,72,1536]{4,3,2,1,0:T(8,128)(2,1)}, bf16[1,1,1,72,1536]{4,3,2,1,0:T(8,128)(2,1)S(1)}, u32[]{:S(2)}, u32[]{:S(2)}) collective-permute-start(bf16[1,1,1,72,1536]{4,3,2,1,0:T(8,128)(2,1)} %maximum_bitcast_fusion.1), channel_id=1, source_target_pairs={{0,8},{1,9},{2,10},{3,11},{4,12},{5,13},{6,14},{7,15},{8,16},{9,17... | collective-permute-start | bytes 663560 | tf_op jit(solution)/shard_map/ppermute | solution.py:41
  28.4 21.7 %collective-permute-start.14 = (bf16[1,1,1,72,1536]{4,3,2,1,0:T(8,128)(2,1)}, bf16[1,1,1,72,1536]{4,3,2,1,0:T(8,128)(2,1)S(1)}, u32[]{:S(2)}, u32[]{:S(2)}) collective-permute-start(bf16[1,1,1,72,1536]{4,3,2,1,0:T(8,128)(2,1)} %maximum_bitcast_fusion.1), channel_id=1, source_target_pairs={{0,16},{1,17},{2,18},{3,19},{4,20},{5,21},{6,22},{7,23},{8,24},{9,... | collective-permute-start | bytes 663560 | tf_op jit(solution)/shard_map/ppermute | solution.py:41
  30.4 19.7 %collective-permute-start.15 = (bf16[1,1,1,72,1536]{4,3,2,1,0:T(8,128)(2,1)}, bf16[1,1,1,72,1536]{4,3,2,1,0:T(8,128)(2,1)S(1)}, u32[]{:S(2)}, u32[]{:S(2)}) collective-permute-start(bf16[1,1,1,72,1536]{4,3,2,1,0:T(8,128)(2,1)} %maximum_bitcast_fusion.1), channel_id=1, source_target_pairs={{0,24},{1,25},{2,26},{3,27},{4,28},{5,29},{6,30},{7,31},{8,0},{9,1... | collective-permute-start | bytes 663560 | tf_op jit(solution)/shard_map/ppermute | solution.py:41
  39.1 12.6 %collective-permute-start.12 = (s32[4,3]{1,0:T(4,128)S(1)}, s32[4,3]{1,0:T(4,128)S(1)}, u32[]{:S(2)}, u32[]{:S(2)}) collective-permute-start(s32[4,3]{1,0:T(4,128)S(1)} %slice.495), channel_id=1, source_target_pairs={{0,4},{1,5},{2,6},{3,7},{4,8},{5,9},{6,10},{7,11},{8,12},{9,13},{1... | collective-permute-start | bytes 152 | tf_op jit(solution)/shard_map/ppermute | solution.py:49
  51.7 14.7 %collective-permute-start.16 = (bf16[4,1,1,72,768]{4,3,2,1,0:T(8,128)(2,1)}, bf16[4,1,1,72,768]{4,3,2,1,0:T(8,128)(2,1)S(1)}, u32[]{:S(2)}, u32[]{:S(2)}) collective-permute-start(bf16[4,1,1,72,768]{4,3,2,1,0:T(8,128)(2,1)} %get-tuple-element.252), channel_id=1, source_target_pairs={{0,4},{1,5},{2,6},{3,7},{4,0},{5,1},{6,2},{7,3},{8,12},{9,13},{10,... | collective-permute-start | bytes 1327112 | tf_op jit(solution)/shard_map/ppermute | solution.py:41
  52.6 18.1 %collective-permute-start.17 = (bf16[4,1,1,72,768]{4,3,2,1,0:T(8,128)(2,1)S(1)}, bf16[4,1,1,72,768]{4,3,2,1,0:T(8,128)(2,1)}, u32[]{:S(2)}, u32[]{:S(2)}) collective-permute-start(bf16[4,1,1,72,768]{4,3,2,1,0:T(8,128)(2,1)S(1)} %get-tuple-element.253), channel_id=1, source_target_pairs={{0,2},{1,3},{2,0},{3,1},{4,6},{5,7},{6,4},{7,5},{8,10},{9,11},{10,... | collective-permute-start | bytes 1327112 | tf_op jit(solution)/shard_map/ppermute | solution.py:41
  54.0 24.5 %collective-permute-start.19 = (bf16[1,1,1,64,3072]{4,3,2,1,0:T(8,128)(2,1)}, bf16[1,1,1,64,3072]{4,3,2,1,0:T(8,128)(2,1)}, u32[]{:S(2)}, u32[]{:S(2)}) collective-permute-start(bf16[1,1,1,64,3072]{4,3,2,1,0:T(8,128)(2,1)} %maximum_bitcast_fusion), channel_id=1, source_target_pairs={{0,8},{1,9},{2,10},{3,11},{4,12},{5,13},{6,14},{7,15},{8,16},{9,17... | collective-permute-start | bytes 1179656 | tf_op jit(solution)/shard_map/ppermute | solution.py:41
  60.9 23.7 %collective-permute-start.20 = (bf16[1,1,1,64,3072]{4,3,2,1,0:T(8,128)(2,1)}, bf16[1,1,1,64,3072]{4,3,2,1,0:T(8,128)(2,1)}, u32[]{:S(2)}, u32[]{:S(2)}) collective-permute-start(bf16[1,1,1,64,3072]{4,3,2,1,0:T(8,128)(2,1)} %maximum_bitcast_fusion), channel_id=1, source_target_pairs={{0,24},{1,25},{2,26},{3,27},{4,28},{5,29},{6,30},{7,31},{8,0},{9,1... | collective-permute-start | bytes 1179656 | tf_op jit(solution)/shard_map/ppermute | solution.py:41
  72.2 31.6 %collective-permute-start.18 = (bf16[4,2,1,72,768]{4,3,2,1,0:T(8,128)(2,1)S(1)}, bf16[4,2,1,72,768]{4,3,2,1,0:T(8,128)(2,1)}, u32[]{:S(2)}, u32[]{:S(2)}) collective-permute-start(bf16[4,2,1,72,768]{4,3,2,1,0:T(8,128)(2,1)S(1)} %pad_maximum_fusion.3.refs_0_), channel_id=1, source_target_pairs={{0,2},{1,3},{2,0},{3,1},{4,6},{5,7},{6,4},{7,5},{8,10},{9,11},{10,... | collective-permute-start | bytes 2654216 | tf_op jit(solution)/shard_map/ppermute | solution.py:41
  73.7 33.7 %collective-permute-start.21 = (bf16[4,1,2,72,768]{4,3,2,1,0:T(8,128)(2,1)}, bf16[4,1,2,72,768]{4,3,2,1,0:T(8,128)(2,1)}, u32[]{:S(2)}, u32[]{:S(2)}) collective-permute-start(bf16[4,1,2,72,768]{4,3,2,1,0:T(8,128)(2,1)} %pad_maximum_fusion.4.refs_2_), channel_id=1, source_target_pairs={{0,4},{1,5},{2,6},{3,7},{4,0},{5,1},{6,2},{7,3},{8,12},{9,13},{10,... | collective-permute-start | bytes 2654216 | tf_op jit(solution)/shard_map/ppermute | solution.py:41
  84.6 26.8 %collective-permute-start.23 = (bf16[1,1,1,64,3072]{4,3,2,1,0:T(8,128)(2,1)}, bf16[1,1,1,64,3072]{4,3,2,1,0:T(8,128)(2,1)S(1)}, u32[]{:S(2)}, u32[]{:S(2)}) collective-permute-start(bf16[1,1,1,64,3072]{4,3,2,1,0:T(8,128)(2,1)} %collective-permute-done.19), channel_id=1, source_target_pairs={{0,8},{1,9},{2,10},{3,11},{4,12},{5,13},{6,14},{7,15},{8,16},{9,17... | collective-permute-start | bytes 1179656 | tf_op jit(solution)/shard_map/ppermute | solution.py:41
  116.2 28.7 %collective-permute-start.29 = (bf16[4,1,1,64,1536]{4,3,2,1,0:T(8,128)(2,1)}, bf16[4,1,1,64,1536]{4,3,2,1,0:T(8,128)(2,1)}, u32[]{:S(2)}, u32[]{:S(2)}) collective-permute-start(bf16[4,1,1,64,1536]{4,3,2,1,0:T(8,128)(2,1)} %get-tuple-element.267), channel_id=1, source_target_pairs={{0,2},{1,3},{2,0},{3,1},{4,6},{5,7},{6,4},{7,5},{8,10},{9,11},{10,... | collective-permute-start | bytes 2359304 | tf_op jit(solution)/shard_map/ppermute | solution.py:41
  117.5 27.5 %collective-permute-start.30 = (bf16[4,1,1,64,1536]{4,3,2,1,0:T(8,128)(2,1)}, bf16[4,1,1,64,1536]{4,3,2,1,0:T(8,128)(2,1)}, u32[]{:S(2)}, u32[]{:S(2)}) collective-permute-start(bf16[4,1,1,64,1536]{4,3,2,1,0:T(8,128)(2,1)} %get-tuple-element.266), channel_id=1, source_target_pairs={{0,4},{1,5},{2,6},{3,7},{4,0},{5,1},{6,2},{7,3},{8,12},{9,13},{10,... | collective-permute-start | bytes 2359304 | tf_op jit(solution)/shard_map/ppermute | solution.py:41
  148.3 35.1 %collective-permute-start.33 = (bf16[4,2,1,64,1536]{4,3,2,1,0:T(8,128)(2,1)}, bf16[4,2,1,64,1536]{4,3,2,1,0:T(8,128)(2,1)}, u32[]{:S(2)}, u32[]{:S(2)}) collective-permute-start(bf16[4,2,1,64,1536]{4,3,2,1,0:T(8,128)(2,1)} %pad_maximum_fusion.1.refs_0_), channel_id=1, source_target_pairs={{0,2},{1,3},{2,0},{3,1},{4,6},{5,7},{6,4},{7,5},{8,10},{9,11},{10,... | collective-permute-start | bytes 4718600 | tf_op jit(solution)/shard_map/ppermute | solution.py:41
  150.8 35.0 %collective-permute-start.32 = (bf16[4,1,2,64,1536]{4,3,2,1,0:T(8,128)(2,1)}, bf16[4,1,2,64,1536]{4,3,2,1,0:T(8,128)(2,1)}, u32[]{:S(2)}, u32[]{:S(2)}) collective-permute-start(bf16[4,1,2,64,1536]{4,3,2,1,0:T(8,128)(2,1)} %pad_maximum_fusion.2.refs_2_), channel_id=1, source_target_pairs={{0,4},{1,5},{2,6},{3,7},{4,0},{5,1},{6,2},{7,3},{8,12},{9,13},{10,... | collective-permute-start | bytes 4718600 | tf_op jit(solution)/shard_map/ppermute | solution.py:41
  150.8 12.4 %collective-permute-start.27 = (f32[8,768]{1,0:T(8,128)S(1)}, f32[8,768]{1,0:T(8,128)S(1)}, u32[]{:S(2)}, u32[]{:S(2)}) collective-permute-start(f32[8,768]{1,0:T(8,128)S(1)} %pad_maximum_fusion.24), channel_id=1, source_target_pairs={{0,12},{1,13},{2,14},{3,15},{4,16},{5,17},{6,18},{7,19},{8,20},{9,... | collective-permute-start | bytes 73736 | tf_op jit(solution)/shard_map/ppermute | solution.py:49
  170.6 15.2 %collective-permute-start.31 = (f32[256,1024]{1,0:T(8,128)}, f32[256,1024]{1,0:T(8,128)S(1)}, u32[]{:S(2)}, u32[]{:S(2)}) collective-permute-start(f32[256,1024]{1,0:T(8,128)} %get-tuple-element.289), channel_id=1, source_target_pairs={{0,1},{1,0},{2,3},{3,2},{4,5},{5,4},{6,7},{7,6},{8,9},{9,8},{10,11... | collective-permute-start | bytes 3145736 | tf_op jit(solution)/shard_map/ppermute | solution.py:41
  217.1 11.4 %collective-permute-start.37 = (bf16[8,96,1024]{2,1,0:T(8,128)(2,1)}, bf16[8,96,1024]{2,1,0:T(8,128)(2,1)}, u32[]{:S(2)}, u32[]{:S(2)}) collective-permute-start(bf16[8,96,1024]{2,1,0:T(8,128)(2,1)} %get-tuple-element.310), channel_id=1, source_target_pairs={{0,1},{1,0},{2,3},{3,2},{4,5},{5,4},{6,7},{7,6},{8,9},{9,8},{10,11... | collective-permute-start | bytes 4718600 | tf_op jit(solution)/shard_map/ppermute | solution.py:41
  217.7 46.8 %collective-permute-start.43 = (bf16[2,4,64,1536]{3,2,1,0:T(8,128)(2,1)}, bf16[2,4,64,1536]{3,2,1,0:T(8,128)(2,1)}, u32[]{:S(2)}, u32[]{:S(2)}) collective-permute-start(bf16[2,4,64,1536]{3,2,1,0:T(8,128)(2,1)} %bitcast.319), channel_id=1, source_target_pairs={{0,2},{1,3},{2,0},{3,1},{4,6},{5,7},{6,4},{7,5},{8,10},{9,11},{10,... | collective-permute-start | bytes 4718600 | tf_op jit(solution)/shard_map/ppermute | solution.py:41
  218.5 46.0 %collective-permute-start.42 = (bf16[2,4,64,1536]{3,2,1,0:T(8,128)(2,1)}, bf16[2,4,64,1536]{3,2,1,0:T(8,128)(2,1)}, u32[]{:S(2)}, u32[]{:S(2)}) collective-permute-start(bf16[2,4,64,1536]{3,2,1,0:T(8,128)(2,1)} %bitcast.318), channel_id=1, source_target_pairs={{0,4},{1,5},{2,6},{3,7},{4,0},{5,1},{6,2},{7,3},{8,12},{9,13},{10,... | collective-permute-start | bytes 4718600 | tf_op jit(solution)/shard_map/ppermute | solution.py:41
  230.5 21.4 %collective-permute-start.38 = (bf16[2,2,96,1024]{3,2,1,0:T(8,128)(2,1)S(1)}, bf16[2,2,96,1024]{3,2,1,0:T(8,128)(2,1)S(1)}, u32[]{:S(2)}, u32[]{:S(2)}) collective-permute-start(bf16[2,2,96,1024]{3,2,1,0:T(8,128)(2,1)S(1)} %get-tuple-element.317), channel_id=1, source_target_pairs={{0,8},{1,9},{2,10},{3,11},{4,12},{5,13},{6,14},{7,15},{8,16},{9,17... | collective-permute-start | bytes 2359304 | tf_op jit(solution)/shard_map/ppermute | solution.py:41
  252.0 16.2 %collective-permute-start.39 = (f32[8,768]{1,0:T(8,128)S(1)}, f32[8,768]{1,0:T(8,128)S(1)}, u32[]{:S(2)}, u32[]{:S(2)}) collective-permute-start(f32[8,768]{1,0:T(8,128)S(1)} %get-tuple-element.326), channel_id=1, source_target_pairs={{4,0},{5,1},{6,2},{7,3},{8,4},{9,5},{10,6},{11,7},{12,8},{13,9},{1... | collective-permute-start | bytes 73736 | tf_op jit(solution)/shard_map/ppermute | solution.py:49
  253.3 14.9 %collective-permute-start.40 = (f32[8,768]{1,0:T(8,128)S(1)}, f32[8,768]{1,0:T(8,128)S(1)}, u32[]{:S(2)}, u32[]{:S(2)}) collective-permute-start(f32[8,768]{1,0:T(8,128)S(1)} %get-tuple-element.326), channel_id=1, source_target_pairs={{8,0},{9,1},{10,2},{11,3},{12,4},{13,5},{14,6},{15,7},{16,8},{17,9... | collective-permute-start | bytes 73736 | tf_op jit(solution)/shard_map/ppermute | solution.py:49
  254.6 17.0 %collective-permute-start.41 = (f32[8,768]{1,0:T(8,128)S(1)}, f32[8,768]{1,0:T(8,128)S(1)}, u32[]{:S(2)}, u32[]{:S(2)}) collective-permute-start(f32[8,768]{1,0:T(8,128)S(1)} %get-tuple-element.326), channel_id=1, source_target_pairs={{12,0},{13,1},{14,2},{15,3},{16,4},{17,5},{18,6},{19,7},{20,8},{21... | collective-permute-start | bytes 73736 | tf_op jit(solution)/shard_map/ppermute | solution.py:49
  275.6 19.8 %collective-permute-start.47 = (bf16[4,64,1536]{2,1,0:T(8,128)(2,1)S(1)}, bf16[4,64,1536]{2,1,0:T(8,128)(2,1)}, u32[]{:S(2)}, u32[]{:S(2)}) collective-permute-start(bf16[4,64,1536]{2,1,0:T(8,128)(2,1)S(1)} %get-tuple-element.336), channel_id=1, source_target_pairs={{0,2},{1,3},{2,0},{3,1},{4,6},{5,7},{6,4},{7,5},{8,10},{9,11},{10,... | collective-permute-start | bytes 2359304 | tf_op jit(solution)/shard_map/ppermute | solution.py:41
  276.4 19.0 %collective-permute-start.48 = (bf16[4,64,1536]{2,1,0:T(8,128)(2,1)S(1)}, bf16[4,64,1536]{2,1,0:T(8,128)(2,1)}, u32[]{:S(2)}, u32[]{:S(2)}) collective-permute-start(bf16[4,64,1536]{2,1,0:T(8,128)(2,1)S(1)} %get-tuple-element.334), channel_id=1, source_target_pairs={{0,4},{1,5},{2,6},{3,7},{4,0},{5,1},{6,2},{7,3},{8,12},{9,13},{10,... | collective-permute-start | bytes 2359304 | tf_op jit(solution)/shard_map/ppermute | solution.py:41
  282.7 18.0 %collective-permute-start.46 = (bf16[2,2,96,1024]{3,2,1,0:T(8,128)(2,1)}, bf16[2,2,96,1024]{3,2,1,0:T(8,128)(2,1)}, u32[]{:S(2)}, u32[]{:S(2)}) collective-permute-start(bf16[2,2,96,1024]{3,2,1,0:T(8,128)(2,1)} %fusion.3), channel_id=1, source_target_pairs={{0,8},{1,9},{2,10},{3,11},{4,12},{5,13},{6,14},{7,15},{8,16},{9,17... | collective-permute-start | bytes 2359304 | tf_op jit(solution)/shard_map/ppermute | solution.py:41
  295.6 16.7 %collective-permute-start.52 = (bf16[2,4,64,768]{3,2,1,0:T(8,128)(2,1)S(1)}, bf16[2,4,64,768]{3,2,1,0:T(8,128)(2,1)S(1)}, u32[]{:S(2)}, u32[]{:S(2)}) collective-permute-start(bf16[2,4,64,768]{3,2,1,0:T(8,128)(2,1)S(1)} %bitcast.321), channel_id=1, source_target_pairs={{0,4},{1,5},{2,6},{3,7},{4,0},{5,1},{6,2},{7,3},{8,12},{9,13},{10,... | collective-permute-start | bytes 2359304 | tf_op jit(solution)/shard_map/ppermute | solution.py:41
  296.4 15.8 %collective-permute-start.53 = (bf16[2,4,64,768]{3,2,1,0:T(8,128)(2,1)S(1)}, bf16[2,4,64,768]{3,2,1,0:T(8,128)(2,1)S(1)}, u32[]{:S(2)}, u32[]{:S(2)}) collective-permute-start(bf16[2,4,64,768]{3,2,1,0:T(8,128)(2,1)S(1)} %bitcast.322), channel_id=1, source_target_pairs={{0,2},{1,3},{2,0},{3,1},{4,6},{5,7},{6,4},{7,5},{8,10},{9,11},{10,... | collective-permute-start | bytes 2359304 | tf_op jit(solution)/shard_map/ppermute | solution.py:41
  306.6 22.2 %collective-permute-start.51 = (bf16[2,2,96,1024]{3,2,1,0:T(8,128)(2,1)S(1)}, bf16[2,2,96,1024]{3,2,1,0:T(8,128)(2,1)S(1)}, u32[]{:S(2)}, u32[]{:S(2)}) collective-permute-start(bf16[2,2,96,1024]{3,2,1,0:T(8,128)(2,1)S(1)} %fusion), channel_id=1, source_target_pairs={{0,8},{1,9},{2,10},{3,11},{4,12},{5,13},{6,14},{7,15},{8,16},{9,17... | collective-permute-start | bytes 2359304 | tf_op jit(solution)/shard_map/ppermute | solution.py:41
  306.7 30.2 %collective-permute-start.50 = (bf16[64,3072]{1,0:T(8,128)(2,1)S(1)}, bf16[64,3072]{1,0:T(8,128)(2,1)S(1)}, u32[]{:S(2)}, u32[]{:S(2)}) collective-permute-start(bf16[64,3072]{1,0:T(8,128)(2,1)S(1)} %pad_maximum_fusion.7), channel_id=1, source_target_pairs={{0,8},{1,9},{2,10},{3,11},{4,12},{5,13},{6,14},{7,15},{8,16},{9,17... | collective-permute-start | bytes 1179656 | tf_op jit(solution)/shard_map/ppermute | solution.py:41
  312.7 26.5 %collective-permute-start.55 = (bf16[2,4,48,768]{3,2,1,0:T(8,128)(2,1)S(1)}, bf16[2,4,48,768]{3,2,1,0:T(8,128)(2,1)S(1)}, u32[]{:S(2)}, u32[]{:S(2)}) collective-permute-start(bf16[2,4,48,768]{3,2,1,0:T(8,128)(2,1)S(1)} %get-tuple-element.375), channel_id=1, source_target_pairs={{0,4},{1,5},{2,6},{3,7},{4,0},{5,1},{6,2},{7,3},{8,12},{9,13},{10,... | collective-permute-start | bytes 1769480 | tf_op jit(solution)/shard_map/ppermute | solution.py:41
  313.8 25.4 %collective-permute-start.56 = (bf16[2,4,48,640]{3,2,1,0:T(8,128)(2,1)S(1)}, bf16[2,4,48,640]{3,2,1,0:T(8,128)(2,1)S(1)}, u32[]{:S(2)}, u32[]{:S(2)}) collective-permute-start(bf16[2,4,48,640]{3,2,1,0:T(8,128)(2,1)S(1)} %get-tuple-element.374), channel_id=1, source_target_pairs={{0,2},{1,3},{2,0},{3,1},{4,6},{5,7},{6,4},{7,5},{8,10},{9,11},{10,... | collective-permute-start | bytes 1474568 | tf_op jit(solution)/shard_map/ppermute | solution.py:41
  314.5 24.6 %collective-permute-start.57 = (bf16[4,64,768]{2,1,0:T(8,128)(2,1)S(1)}, bf16[4,64,768]{2,1,0:T(8,128)(2,1)S(1)}, u32[]{:S(2)}, u32[]{:S(2)}) collective-permute-start(bf16[4,64,768]{2,1,0:T(8,128)(2,1)S(1)} %get-tuple-element.373), channel_id=1, source_target_pairs={{0,2},{1,3},{2,0},{3,1},{4,6},{5,7},{6,4},{7,5},{8,10},{9,11},{10,... | collective-permute-start | bytes 1179656 | tf_op jit(solution)/shard_map/ppermute | solution.py:41
  345.7 14.1 %collective-permute-start.60 = (bf16[64,3072]{1,0:T(8,128)(2,1)}, bf16[64,3072]{1,0:T(8,128)(2,1)}, u32[]{:S(2)}, u32[]{:S(2)}) collective-permute-start(bf16[64,3072]{1,0:T(8,128)(2,1)} %add_convert_fusion.1), channel_id=1, source_target_pairs={{0,8},{1,9},{2,10},{3,11},{4,12},{5,13},{6,14},{7,15},{8,16},{9,17... | collective-permute-start | bytes 1179656 | tf_op jit(solution)/shard_map/ppermute | solution.py:41
  348.0 21.0 %collective-permute-start.62 = (bf16[4,48,768]{2,1,0:T(8,128)(2,1)}, bf16[4,48,768]{2,1,0:T(8,128)(2,1)}, u32[]{:S(2)}, u32[]{:S(2)}) collective-permute-start(bf16[4,48,768]{2,1,0:T(8,128)(2,1)} %get-tuple-element.389), channel_id=1, source_target_pairs={{0,2},{1,3},{2,0},{3,1},{4,6},{5,7},{6,4},{7,5},{8,10},{9,11},{10,... | collective-permute-start | bytes 884744 | tf_op jit(solution)/shard_map/ppermute | solution.py:41
  348.8 20.2 %collective-permute-start.63 = (bf16[4,48,640]{2,1,0:T(8,128)(2,1)}, bf16[4,48,640]{2,1,0:T(8,128)(2,1)}, u32[]{:S(2)}, u32[]{:S(2)}) collective-permute-start(bf16[4,48,640]{2,1,0:T(8,128)(2,1)} %get-tuple-element.387), channel_id=1, source_target_pairs={{0,4},{1,5},{2,6},{3,7},{4,0},{5,1},{6,2},{7,3},{8,12},{9,13},{10,... | collective-permute-start | bytes 737288 | tf_op jit(solution)/shard_map/ppermute | solution.py:41
  349.1 15.1 %collective-permute-start.64 = (bf16[64,1536]{1,0:T(8,128)(2,1)}, bf16[64,1536]{1,0:T(8,128)(2,1)S(1)}, u32[]{:S(2)}, u32[]{:S(2)}) collective-permute-start(bf16[64,1536]{1,0:T(8,128)(2,1)} %pad_maximum_fusion.13), channel_id=1, source_target_pairs={{0,24},{1,25},{2,26},{3,27},{4,28},{5,29},{6,30},{7,31},{8,0},{9,1... | collective-permute-start | bytes 589832 | tf_op jit(solution)/shard_map/ppermute | solution.py:41
  355.3 12.4 %collective-permute-start.65 = (bf16[64,1536]{1,0:T(8,128)(2,1)S(1)}, bf16[64,1536]{1,0:T(8,128)(2,1)S(1)}, u32[]{:S(2)}, u32[]{:S(2)}) collective-permute-start(bf16[64,1536]{1,0:T(8,128)(2,1)S(1)} %copy-done.73), channel_id=1, source_target_pairs={{0,8},{1,9},{2,10},{3,11},{4,12},{5,13},{6,14},{7,15},{8,16},{9,17... | collective-permute-start | bytes 589832 | tf_op jit(solution)/shard_map/ppermute | solution.py:41
  359.8 11.3 %collective-permute-start.61 = (bf16[2,96,1024]{2,1,0:T(8,128)(2,1)}, bf16[2,96,1024]{2,1,0:T(8,128)(2,1)S(1)}, u32[]{:S(2)}, u32[]{:S(2)}) collective-permute-start(bf16[2,96,1024]{2,1,0:T(8,128)(2,1)} %get-tuple-element.398), channel_id=1, source_target_pairs={{0,4},{1,5},{2,6},{3,7},{4,0},{5,1},{6,2},{7,3},{8,12},{9,13},{10,... | collective-permute-start | bytes 1179656 | tf_op jit(solution)/shard_map/ppermute | solution.py:41
  364.2 19.3 %collective-permute-start.69 = (bf16[64,3072]{1,0:T(8,128)(2,1)}, bf16[64,3072]{1,0:T(8,128)(2,1)}, u32[]{:S(2)}, u32[]{:S(2)}) collective-permute-start(bf16[64,3072]{1,0:T(8,128)(2,1)} %add_convert_fusion), channel_id=1, source_target_pairs={{0,8},{1,9},{2,10},{3,11},{4,12},{5,13},{6,14},{7,15},{8,16},{9,17... | collective-permute-start | bytes 1179656 | tf_op jit(solution)/shard_map/ppermute | solution.py:41
  368.8 12.4 %collective-permute-start.70 = (bf16[64,1536]{1,0:T(8,128)(2,1)}, bf16[64,1536]{1,0:T(8,128)(2,1)S(1)}, u32[]{:S(2)}, u32[]{:S(2)}) collective-permute-start(bf16[64,1536]{1,0:T(8,128)(2,1)} %add_convert_fusion.6), channel_id=1, source_target_pairs={{0,24},{1,25},{2,26},{3,27},{4,28},{5,29},{6,30},{7,31},{8,0},{9,1... | collective-permute-start | bytes 589832 | tf_op jit(solution)/shard_map/ppermute | solution.py:41
  372.9 15.6 %collective-permute-start.72 = (bf16[96,1024]{1,0:T(8,128)(2,1)S(1)}, bf16[96,1024]{1,0:T(8,128)(2,1)S(1)}, u32[]{:S(2)}, u32[]{:S(2)}) collective-permute-start(bf16[96,1024]{1,0:T(8,128)(2,1)S(1)} %fusion.22), channel_id=1, source_target_pairs={{0,2},{1,3},{2,0},{3,1},{4,6},{5,7},{6,4},{7,5},{8,10},{9,11},{10,... | collective-permute-start | bytes 589832 | tf_op jit(solution)/shard_map/ppermute | solution.py:41
  373.8 12.2 %collective-permute-start.73 = (bf16[48,1408]{1,0:T(8,128)(2,1)S(1)}, bf16[48,1408]{1,0:T(8,128)(2,1)S(1)}, u32[]{:S(2)}, u32[]{:S(2)}) collective-permute-start(bf16[48,1408]{1,0:T(8,128)(2,1)S(1)} %pad_maximum_fusion.17), channel_id=1, source_target_pairs={{0,24},{1,25},{2,26},{3,27},{4,28},{5,29},{6,30},{7,31},{8,0},{9,1... | collective-permute-start | bytes 405512 | tf_op jit(solution)/shard_map/ppermute | solution.py:41
  (118 other events, 1047.9 us)
Sparse Core Ops, SparseCore 0:
  11.5 113.6 all-gather.2
